TPU v7x, 128 devices: a whole 4x4x4 slice. The times are simulated.
128 devices in a mesh: ctx: 32 (over y, z_lo, x), tp: 4 (over z_hi, core).
Axes of the slice: x: 4, y: 4, z: 4 (z_hi: 2, z_lo: 2; z = z_hi * 2 + z_lo), core: 2. Of those that a mesh axis runs over, the one named last changes fastest.
Arguments:
- tokens_in: bfloat16 [8192, 2048], P('ctx'), may hold values from -6 to 6
- w_query: bfloat16 [2048, 2048], P('ctx', 'tp'), may hold values from -0.1875 to 0.1875
- w_key: bfloat16 [2048, 2048], P('ctx', 'tp'), may hold values from -0.1875 to 0.1875
- w_value: bfloat16 [2048, 2048], P('ctx', 'tp'), may hold values from -0.125 to 0.125
- w_output: bfloat16 [2048, 2048], P('ctx', 'tp'), may hold values from -0.75 to 0.75
- w_gate: bfloat16 [2048, 8192], P('ctx', 'tp'), may hold values from -0.125 to 0.125
- w_up: bfloat16 [2048, 8192], P('ctx', 'tp'), may hold values from -0.125 to 0.125
- w_down: bfloat16 [2048, 8192], P('ctx', 'tp'), may hold values from -0.0625 to 0.0625
- grad_out: bfloat16 [8192, 2048], P('ctx'), may hold values from -6 to 6
- block_ids: int32 [2, 4096], replicated, may hold values from 0 to 20, never falling along the last dimension, each value on 1 to 256 neighbouring positions
- tile_order: int32 [2, 64], replicated, may hold values from 0 to 63, as said below
Outputs:
- tokens_out: bfloat16 [8192, 2048], P('ctx')
- grad_in: float32 [8192, 2048], P('ctx')
- grad_query: float32 [2048, 2048], P('ctx', 'tp')
- grad_key: float32 [2048, 2048], P('ctx', 'tp')
- grad_value: float32 [2048, 2048], P('ctx', 'tp')
- grad_output: float32 [2048, 2048], P('ctx', 'tp')
- grad_gate: float32 [2048, 8192], P('ctx', 'tp')
- grad_up: float32 [2048, 8192], P('ctx', 'tp')
- grad_down: float32 [2048, 8192], P('ctx', 'tp')
Inputs may be any that keep to these rules, and one draw needn't show every extreme that they name: `tile_order`: in each row every piece number appears once; columns 2 i and 2 i + 1 hold c and 63 - c with c < 32, the order of the c drawn afresh. `block_ids`: within a sequence the ids never fall and every id occurs; one block has at most 256 positions.
All inputs are finite; a program needn't handle non-finite values.
Results may differ from a plain program's by a relative error of at most 0.035.
Values may be sent and summed in bfloat16 or wider, within the bound.
No kernel may reach another device: no remote copies, remote signals or barrier semaphores. Data moves between devices by JAX's collectives and lax.ppermute only.
A program may use at most 256 MiB of HBM per device.

v0:
```python
import jax
import jax.numpy as jnp
from jax import lax
from jax.sharding import PartitionSpec as P

HEAD_DIM = 128


def side_by_side(arrays, axis, dim, along):
    widths = [a.shape[along] for a in arrays]
    both = jnp.concatenate(arrays, axis=along)
    whole = lax.all_gather(both, axis, axis=dim, tiled=True)
    return tuple(jnp.split(whole, [sum(widths[:k]) for k in range(1, len(widths))], axis=along))


def layer_norm(values):
    average = jnp.mean(values, axis=-1, keepdims=True)
    centred = values - average
    inverse = lax.rsqrt(jnp.mean(centred * centred, axis=-1, keepdims=True) + 1e-05)
    return (centred * inverse, inverse)


def norm_back(grad, normed, inverse):
    first_mean = jnp.mean(grad, axis=-1, keepdims=True)
    second_mean = jnp.mean(grad * normed, axis=-1, keepdims=True)
    return inverse * (grad - first_mean - normed * second_mean)


def tables(positions, head_width):
    inverse = 10000.0 ** (-jnp.arange(0, head_width, 2, dtype=jnp.float32) / head_width)
    angles = positions[:, None] * inverse[None, :]
    angles = jnp.concatenate([angles, angles], axis=-1)
    return (jnp.cos(angles), jnp.sin(angles))


def rotate(values, cosine, sine):
    middle = values.shape[-1] // 2
    turned = jnp.concatenate([-values[..., middle:], values[..., :middle]], axis=-1)
    return values * cosine[:, None, :] + turned * sine[:, None, :]


def local(
    tokens_in,
    w_query,
    w_key,
    w_value,
    w_output,
    w_gate,
    w_up,
    w_down,
    grad_out,
    block_ids,
    tile_order,
):
    token_count, model_width = tokens_in.shape
    seq_count, seq_len = block_ids.shape
    tile_count = tile_order.shape[1]
    tile_len = seq_len // tile_count
    pair_len = 2 * tile_len
    device_count = lax.axis_size("ctx")
    head_width = HEAD_DIM
    heads_width = w_query.shape[1]
    local_heads = heads_width // head_width
    hidden_width = w_gate.shape[1]
    scaling = head_width ** (-0.5)
    own_index = lax.axis_index("ctx")
    own_tiles = lax.dynamic_slice_in_dim(tile_order, 2 * own_index, 2, 1)
    offsets = jnp.arange(tile_len, dtype=jnp.int32)
    own_positions = (own_tiles[:, :, None] * tile_len + offsets).reshape(token_count)
    block_table = block_ids.reshape(seq_count, tile_count, tile_len)
    take_rows = jax.vmap(lambda table_row, order_row: jnp.take(table_row, order_row, axis=0))
    key_blocks = take_rows(block_table, tile_order).reshape(seq_count, seq_len)
    own_blocks = take_rows(block_table, own_tiles).reshape(seq_count, pair_len)
    cosine, sine = tables(own_positions.astype(jnp.float32), head_width)
    inputs = tokens_in.astype(jnp.float32)
    normed_one, inverse_one = layer_norm(inputs)
    first_low = normed_one.astype(jnp.bfloat16)
    attn_weights = side_by_side((w_query, w_key, w_value, w_output), "ctx", 0, 1)

    def project(matrix):
        product = jnp.dot(first_low, matrix, preferred_element_type=jnp.float32)
        return product.reshape(token_count, local_heads, head_width)

    query_rot = rotate(project(attn_weights[0]), cosine, sine).astype(jnp.bfloat16)
    key_rot = rotate(project(attn_weights[1]), cosine, sine).astype(jnp.bfloat16)
    value_low = project(attn_weights[2]).astype(jnp.bfloat16)
    keys_all, values_all = side_by_side(
        (key_rot.reshape(token_count, heads_width), value_low.reshape(token_count, heads_width)),
        "ctx",
        0,
        1,
    )
    keys_seq = keys_all.reshape(device_count, seq_count, pair_len, local_heads, head_width)
    values_seq = values_all.reshape(device_count, seq_count, pair_len, local_heads, head_width)
    query_seq = query_rot.reshape(seq_count, pair_len, local_heads, head_width)

    def seq_keys(position):
        return keys_seq[:, position].reshape(seq_len, local_heads, head_width)

    def seq_values(position):
        return values_seq[:, position].reshape(seq_len, local_heads, head_width)

    def masked_scores(position):
        raw = (
            jnp.einsum(
                "qhd,khd->hqk",
                query_seq[position],
                seq_keys(position),
                preferred_element_type=jnp.float32,
            )
            * scaling
        )
        allowed = own_blocks[position][:, None] >= key_blocks[position][None, :]
        return jnp.where(allowed[None], raw, -1e30)

    attended_list = []
    log_totals = []
    for position in range(seq_count):
        masked = masked_scores(position)
        row_max = jnp.max(masked, axis=-1, keepdims=True)
        exponent = jnp.exp(masked - row_max)
        row_total = jnp.sum(exponent, axis=-1, keepdims=True)
        weights_low = (exponent / row_total).astype(jnp.bfloat16)
        attended_list.append(
            jnp.einsum(
                "hqk,khd->qhd",
                weights_low,
                seq_values(position),
                preferred_element_type=jnp.float32,
            )
        )
        log_totals.append(row_max + jnp.log(row_total))
    attended_low = (
        jnp.concatenate(attended_list, axis=0)
        .reshape(token_count, heads_width)
        .astype(jnp.bfloat16)
    )
    attn_part = jnp.einsum(
        "tc,dc->td", attended_low, attn_weights[3], preferred_element_type=jnp.float32
    )
    middle = inputs + lax.psum(attn_part.astype(jnp.bfloat16), "tp").astype(jnp.float32)
    normed_two, inverse_two = layer_norm(middle)
    second_low = normed_two.astype(jnp.bfloat16)
    mlp_weights = side_by_side((w_gate, w_up, w_down), "ctx", 0, 1)
    gate = jnp.dot(second_low, mlp_weights[0], preferred_element_type=jnp.float32)
    upper = jnp.dot(second_low, mlp_weights[1], preferred_element_type=jnp.float32)
    sigmoid_gate = jax.nn.sigmoid(gate)
    swish = gate * sigmoid_gate
    hidden_low = (swish * upper).astype(jnp.bfloat16)
    mlp_part = jnp.einsum(
        "tf,df->td", hidden_low, mlp_weights[2], preferred_element_type=jnp.float32
    )
    tokens_out = (
        middle + lax.psum(mlp_part.astype(jnp.bfloat16), "tp").astype(jnp.float32)
    ).astype(jnp.bfloat16)
    grad_hidden = jnp.dot(grad_out, mlp_weights[2], preferred_element_type=jnp.float32)
    grad_gate_low = (
        grad_hidden * upper * sigmoid_gate * (1.0 + gate * (1.0 - sigmoid_gate))
    ).astype(jnp.bfloat16)
    grad_up_low = (grad_hidden * swish).astype(jnp.bfloat16)
    back_two = jnp.einsum(
        "tf,df->td", grad_gate_low, mlp_weights[0], preferred_element_type=jnp.float32
    )
    back_two = back_two + jnp.einsum(
        "tf,df->td", grad_up_low, mlp_weights[1], preferred_element_type=jnp.float32
    )
    back_two = lax.psum(back_two.astype(jnp.bfloat16), "tp").astype(jnp.float32)
    grad_middle = grad_out.astype(jnp.float32) + norm_back(back_two, normed_two, inverse_two)
    grad_middle_low = grad_middle.astype(jnp.bfloat16)
    gate_term = jnp.einsum(
        "td,tf->df", second_low, grad_gate_low, preferred_element_type=jnp.float32
    )
    up_term = jnp.einsum("td,tf->df", second_low, grad_up_low, preferred_element_type=jnp.float32)
    down_term = jnp.einsum("td,tf->df", grad_out, hidden_low, preferred_element_type=jnp.float32)
    mlp_grads = lax.psum_scatter(
        jnp.concatenate([gate_term, up_term, down_term], axis=1).astype(jnp.bfloat16),
        "ctx",
        scatter_dimension=0,
        tiled=True,
    ).astype(jnp.float32)
    grad_att_low = jnp.dot(
        grad_middle_low, attn_weights[3], preferred_element_type=jnp.float32
    ).astype(jnp.bfloat16)
    grad_att_seq = grad_att_low.reshape(seq_count, pair_len, local_heads, head_width)
    grad_query_rot = []
    row_deltas = []
    for position in range(seq_count):
        probs = jnp.exp(masked_scores(position) - log_totals[position])
        grad_probs = jnp.einsum(
            "qhd,khd->hqk",
            grad_att_seq[position],
            seq_values(position),
            preferred_element_type=jnp.float32,
        )
        row_delta = jnp.sum(probs * grad_probs, axis=-1, keepdims=True)
        row_deltas.append(row_delta)
        score_low = (probs * (grad_probs - row_delta)).astype(jnp.bfloat16)
        grad_query_rot.append(
            jnp.einsum(
                "hqk,khd->qhd", score_low, seq_keys(position), preferred_element_type=jnp.float32
            )
            * scaling
        )
    query_back = jnp.concatenate(grad_query_rot, axis=0)
    grad_query_low = (
        rotate(query_back, cosine, -sine).astype(jnp.bfloat16).reshape(token_count, heads_width)
    )
    lse_rows = jnp.transpose(jnp.stack(log_totals, axis=0)[..., 0], (0, 2, 1)).reshape(
        token_count, local_heads
    )
    delta_rows = jnp.transpose(jnp.stack(row_deltas, axis=0)[..., 0], (0, 2, 1)).reshape(
        token_count, local_heads
    )
    queries_all, grads_all = side_by_side(
        (query_rot.reshape(token_count, heads_width), grad_att_low), "ctx", 0, 1
    )
    lse_all, delta_all = side_by_side((lse_rows, delta_rows), "ctx", 0, 1)
    queries_grid = queries_all.reshape(device_count, seq_count, pair_len, local_heads, head_width)
    grads_grid = grads_all.reshape(device_count, seq_count, pair_len, local_heads, head_width)
    lse_grid = lse_all.reshape(device_count, seq_count, pair_len, local_heads)
    delta_grid = delta_all.reshape(device_count, seq_count, pair_len, local_heads)
    own_keys = key_rot.reshape(seq_count, pair_len, local_heads, head_width)
    own_values = value_low.reshape(seq_count, pair_len, local_heads, head_width)
    key_list = []
    value_list = []
    for position in range(seq_count):
        queries_full = queries_grid[:, position].reshape(seq_len, local_heads, head_width)
        grads_full = grads_grid[:, position].reshape(seq_len, local_heads, head_width)
        lse_full = jnp.transpose(lse_grid[:, position].reshape(seq_len, local_heads))
        delta_full = jnp.transpose(delta_grid[:, position].reshape(seq_len, local_heads))
        raw = (
            jnp.einsum(
                "qhd,khd->hqk", queries_full, own_keys[position], preferred_element_type=jnp.float32
            )
            * scaling
        )
        allowed = key_blocks[position][:, None] >= own_blocks[position][None, :]
        masked = jnp.where(allowed[None], raw, -1e30)
        probs = jnp.exp(masked - lse_full[:, :, None])
        grad_probs = jnp.einsum(
            "qhd,khd->hqk", grads_full, own_values[position], preferred_element_type=jnp.float32
        )
        score_low = (probs * (grad_probs - delta_full[:, :, None])).astype(jnp.bfloat16)
        prob_low = probs.astype(jnp.bfloat16)
        key_list.append(
            jnp.einsum("hqk,qhd->khd", score_low, queries_full, preferred_element_type=jnp.float32)
            * scaling
        )
        value_list.append(
            jnp.einsum("hqk,qhd->khd", prob_low, grads_full, preferred_element_type=jnp.float32)
        )
    key_back = jnp.concatenate(key_list, axis=0)
    grad_value_low = (
        jnp.concatenate(value_list, axis=0).reshape(token_count, heads_width).astype(jnp.bfloat16)
    )
    grad_key_low = (
        rotate(key_back, cosine, -sine).astype(jnp.bfloat16).reshape(token_count, heads_width)
    )
    back_one = jnp.einsum(
        "tc,dc->td", grad_query_low, attn_weights[0], preferred_element_type=jnp.float32
    )
    back_one = back_one + jnp.einsum(
        "tc,dc->td", grad_key_low, attn_weights[1], preferred_element_type=jnp.float32
    )
    back_one = back_one + jnp.einsum(
        "tc,dc->td", grad_value_low, attn_weights[2], preferred_element_type=jnp.float32
    )
    back_one = lax.psum(back_one.astype(jnp.bfloat16), "tp").astype(jnp.float32)
    grad_in = grad_middle + norm_back(back_one, normed_one, inverse_one)
    query_term = jnp.einsum(
        "td,tc->dc", first_low, grad_query_low, preferred_element_type=jnp.float32
    )
    key_term = jnp.einsum("td,tc->dc", first_low, grad_key_low, preferred_element_type=jnp.float32)
    value_term = jnp.einsum(
        "td,tc->dc", first_low, grad_value_low, preferred_element_type=jnp.float32
    )
    output_term = jnp.einsum(
        "td,tc->dc", grad_middle_low, attended_low, preferred_element_type=jnp.float32
    )
    attn_grads = lax.psum_scatter(
        jnp.concatenate([query_term, key_term, value_term, output_term], axis=1).astype(
            jnp.bfloat16
        ),
        "ctx",
        scatter_dimension=0,
        tiled=True,
    ).astype(jnp.float32)
    grad_query = attn_grads[:, :heads_width]
    grad_key = attn_grads[:, heads_width : 2 * heads_width]
    grad_value = attn_grads[:, 2 * heads_width : 3 * heads_width]
    grad_output = attn_grads[:, 3 * heads_width :]
    grad_gate = mlp_grads[:, :hidden_width]
    grad_up = mlp_grads[:, hidden_width : 2 * hidden_width]
    grad_down = mlp_grads[:, 2 * hidden_width :]
    return (
        tokens_out,
        grad_in,
        grad_query,
        grad_key,
        grad_value,
        grad_output,
        grad_gate,
        grad_up,
        grad_down,
    )


def solution(mesh):
    return jax.shard_map(
        local,
        mesh=mesh,
        in_specs=(
            P("ctx", None),
            P("ctx", "tp"),
            P("ctx", "tp"),
            P("ctx", "tp"),
            P("ctx", "tp"),
            P("ctx", "tp"),
            P("ctx", "tp"),
            P("ctx", "tp"),
            P("ctx", None),
            P(),
            P(),
        ),
        out_specs=(
            P("ctx", None),
            P("ctx", None),
            P("ctx", "tp"),
            P("ctx", "tp"),
            P("ctx", "tp"),
            P("ctx", "tp"),
            P("ctx", "tp"),
            P("ctx", "tp"),
            P("ctx", "tp"),
        ),
        check_vma=False,
    )
```

profile of v0, /device:TPU:0, one launch (start us, length us, event | category | flops | bytes accessed | tf_op | source)
XLA Modules:
  0.0 1618.0 jit_solution(6997082612571053943)
XLA Ops:
  13.8 165.9 %all-gather.5.cloned.1.call-done = bf16[2048,2048]{1,0:T(8,128)(2,1)} async-done(((bf16[64,2048]{1,0:T(8,128)(2,1)}), bf16[2048,2048]{1,0:T(8,128)(2,1)}) %all-gather.5.cloned.1.call-update) | async-done | bytes 8388624 | tf_op jit(solution)/shard_map/all_gather | solution.py:12
  179.7 2.7 fusion.60
  182.4 2.3 fusion.64
  186.6 2.4 fusion.70
  194.6 189.9 %all-gather.7.cloned.1.call-done = bf16[8192,1024]{1,0:T(8,128)(2,1)} async-done(((bf16[256,1024]{1,0:T(8,128)(2,1)}), bf16[8192,1024]{1,0:T(8,128)(2,1)}) %all-gather.7.cloned.1.call-update) | async-done | bytes 16777232 | tf_op jit(solution)/shard_map/all_gather | solution.py:12
  384.5 11.5 fusion.144
  396.1 12.5 reshape.441
  408.6 5.6 fusion.147
  414.3 3.1 copy.110
  417.4 3.1 copy.112
  420.5 12.6 reshape.438
  433.0 5.6 fusion.148
  438.7 3.0 copy.106
  447.6 3.9 copy-done.7
  454.7 3.0 copy-done.3
  458.7 2.1 fusion.94
  460.9 2.1 fusion.95
  463.2 3.5 convolution_convert_fusion.6
  467.3 195.3 %all-gather.9.cloned.1.call-done = bf16[2048,6144]{1,0:T(8,128)(2,1)} async-done(((bf16[64,6144]{1,0:T(8,128)(2,1)}), bf16[2048,6144]{1,0:T(8,128)(2,1)}) %all-gather.9.cloned.1.call-update) | async-done | bytes 25165840 | tf_op jit(solution)/shard_map/all_gather | solution.py:12
  662.6 7.0 fusion.26
  669.6 37.7 %all-reduce.5.cloned.1.call-done = bf16[256,2048]{1,0:T(8,128)(2,1)} async-done(((bf16[256,2048]{1,0:T(8,128)(2,1)}), bf16[256,2048]{1,0:T(8,128)(2,1)}) %all-reduce.5.cloned.1.call-update) | async-done | bytes 1048592 | tf_op jit(solution)/shard_map/psum | solution.py:141
  711.7 5.9 fusion.8
  717.6 7.5 multiply_convert_fusion.7
  725.1 6.5 fusion.6
  731.7 6.7 fusion.32
  738.6 45.0 %all-reduce.7.cloned.1.call-done = bf16[256,2048]{1,0:T(8,128)(2,1)} async-done(((bf16[256,2048]{1,0:T(8,128)(2,1)}), bf16[256,2048]{1,0:T(8,128)(2,1)}) %all-reduce.7.cloned.1.call-update) | async-done | bytes 1048592 | tf_op jit(solution)/shard_map/psum | solution.py:167
  785.7 2.5 fusion.49
  789.7 2.4 fusion.73
  793.2 2.6 broadcast_compare_fusion
  795.7 2.5 broadcast_compare_fusion.1
  798.4 7.0 convolution_convert_fusion.1
  805.3 5.6 convolution_convert_fusion
  811.0 7.0 fusion.36
  818.6 4.1 multiply_reduce_fusion.1
  822.7 5.0 fusion.77
  828.5 9.6 multiply_reduce_fusion
  838.1 83.9 %all_gather.19 = f32[8192,8]{0,1:T(8,128)S(1)} all-gather(f32[256,8]{0,1:T(8,128)S(1)} %pad_maximum_fusion.11), channel_id=1, replica_groups=mesh['ctx'=32,'tp'=4] {'ctx'}, dimensions={0}, use_global_device_ids=true | all-gather | bytes 270336 | tf_op jit(solution)/shard_map/all_gather | solution.py:12
  923.2 9.7 fusion.76
  933.8 53.8 %all-gather.11.cloned.1.call-done = bf16[8192,1024]{1,0:T(8,128)(2,1)} async-done(((bf16[256,1024]{1,0:T(8,128)(2,1)}), bf16[8192,1024]{1,0:T(8,128)(2,1)}) %all-gather.11.cloned.1.call-update) | async-done | bytes 16777232 | tf_op jit(solution)/shard_map/all_gather | solution.py:12
  987.5 11.4 fusion.143
  998.9 12.6 reshape.446
  1011.5 5.6 fusion.145
  1017.1 3.1 copy.126
  1020.2 3.1 copy.131
  1023.3 12.5 reshape.442
  1035.8 5.6 fusion.146
  1041.4 3.2 copy.124
  1045.7 2.5 subtract_exponential_fusion
  1051.5 7.8 fusion.78
  1060.2 6.8 subtract_exponential_fusion.1
  1070.5 7.9 fusion.79
  1083.1 2.4 fusion.62
  1085.5 2.3 convolution_add_fusion.1
  1087.9 3.5 fusion.35
  1091.5 5.7 convert_bitcast_fusion
  1097.2 18.6 %pad_maximum_fusion = bf16[2048,6144]{0,1:T(8,128)(2,1)} fusion(bf16[2048,2048]{0,1:T(8,128)(2,1)} %convert_bitcast_fusion, bf16[2048,2048]{0,1:T(8,128)(2,1)} %convolution_convert_fusion, bf16[2048,2048]{0,1:T(8,128)(2,1)} %convolution_convert_fusion.1), kind=kLoop, calls=%fused_computation.2 | loop fusion | flops 75497472 | bytes 50331648 | tf_op jit(solution)/shard_map/concatenate | solution.py:176
  1115.8 32.9 %copy.161 = bf16[2048,6144]{1,0:T(8,128)(2,1)} copy(bf16[2048,6144]{0,1:T(8,128)(2,1)} %pad_maximum_fusion) | data formatting | bytes 50331648
  1154.6 4.1 pad_maximum_fusion.1
  1158.7 11.8 copy.159
  1172.6 4.9 fusion.45
  1177.5 250.7 %reduce-scatter.9.cloned.1.call-done = bf16[64,6144]{1,0:T(8,128)(2,1)} async-done(((bf16[2048,6144]{1,0:T(8,128)(2,1)}), bf16[64,6144]{1,0:T(8,128)(2,1)}) %reduce-scatter.9.cloned.1.call-update) | async-done | bytes 786448
  1431.6 2.3 copy.145
  1433.9 2.3 copy.144
  1437.4 169.5 %reduce-scatter.7.cloned.1.call-done = bf16[64,2048]{1,0:T(8,128)(2,1)} async-done(((bf16[2048,2048]{1,0:T(8,128)(2,1)}), bf16[64,2048]{1,0:T(8,128)(2,1)}) %reduce-scatter.7.cloned.1.call-update) | async-done | bytes 262160
  (252 shorter events, 67.2 us)
Async XLA Ops:
  7.2 172.5 %all-gather.5.cloned.1.call-start = ((), (), s32[]{:S(2)}) async-start(), calls=%async_computation.2 | async-start | bytes 8650752 | tf_op jit(solution)/shard_map/all_gather | solution.py:12
  8.9 375.6 %all-gather.7.cloned.1.call-start = ((), (), s32[]{:S(2)}) async-start(), calls=%async_computation.3 | async-start | bytes 17301504 | tf_op jit(solution)/shard_map/all_gather | solution.py:12
  10.5 171.9 %copy-start = (bf16[256,2048]{1,0:T(8,128)(2,1)S(1)}, bf16[256,2048]{1,0:T(8,128)(2,1)}, u32[]{:S(2)}) copy-start(bf16[256,2048]{1,0:T(8,128)(2,1)} %param.11) | copy-start | bytes 3145732
  12.1 174.4 %copy-start.43 = (f32[256]{0:T(256)}, f32[256]{0:T(256)S(1)}, u32[]{:S(2)}) copy-start(f32[256]{0:T(256)S(1)} %broadcast_multiply_fusion.6) | copy-start | bytes 3076
  13.8 172.8 %copy-start.45 = (f32[256]{0:T(256)}, f32[256]{0:T(256)S(1)}, u32[]{:S(2)}) copy-start(f32[256]{0:T(256)S(1)} %add_rsqrt_fusion.1) | copy-start | bytes 3076
  186.3 2.8 copy-start.19
  186.6 3.5 copy-start.38
  186.6 3.5 copy-start.39
  186.6 3.5 copy-start.40
  186.6 4.5 copy-start.53
  186.6 4.7 copy-start.47
  189.1 207.0 %copy-start.33 = (bf16[256,512]{1,0:T(8,128)(2,1)}, bf16[256,512]{1,0:T(8,128)(2,1)S(1)}, u32[]{:S(2)}) copy-start(bf16[256,512]{1,0:T(8,128)(2,1)S(1)} %fusion.70) | copy-start | bytes 786436
  190.0 472.6 %all-gather.9.cloned.1.call-start = ((), (), s32[]{:S(2)}) async-start(), calls=%async_computation.5 | async-start | bytes 25952256 | tf_op jit(solution)/shard_map/all_gather | solution.py:12
  191.0 516.3 %all-reduce.5.cloned.1.call-start = ((), (), s32[]{:S(2)}) async-start(), calls=%async_computation.4 | async-start | bytes 2097152 | tf_op jit(solution)/shard_map/psum | solution.py:141
  193.5 202.6 %copy-start.59 = (s32[128]{0:T(128)}, s32[128]{0:T(128)S(1)}, u32[]{:S(2)}) copy-start(s32[128]{0:T(128)S(1)} %ge.103) | copy-start | bytes 1540
  193.8 202.3 %copy-start.61 = (s32[128]{0:T(128)}, s32[128]{0:T(128)S(1)}, u32[]{:S(2)}) copy-start(s32[128]{0:T(128)S(1)} %ge.109) | copy-start | bytes 1540
  193.8 202.2 %copy-start.41 = (s32[4096]{0:T(1024)}, s32[4096]{0:T(1024)S(1)}, u32[]{:S(2)}) copy-start(s32[4096]{0:T(1024)S(1)} %ge.111) | copy-start | bytes 49156
  442.8 18.0 %copy-start.15 = (bf16[32,1,128,4,128]{4,2,0,3,1:T(8,128)(2,1)}, bf16[32,1,128,4,128]{4,2,0,3,1:T(8,128)(2,1)S(1)}, u32[]{:S(2)}) copy-start(bf16[32,1,128,4,128]{4,2,0,3,1:T(8,128)(2,1)S(1)} %copy.111) | copy-start | bytes 12582916
  446.3 14.6 copy-start.2
  446.3 14.6 copy-start.49
  446.3 5.2 copy-start.7
  447.6 13.3 copy-start.55
  453.4 4.3 copy-start.3
  453.4 4.3 copy-start.51
  453.4 5.2 copy-start.16
  454.7 6.1 copy-start.57
  463.0 199.6 %copy-start.21 = (bf16[256,2048]{1,0:T(8,128)(2,1)S(1)}, bf16[256,2048]{1,0:T(8,128)(2,1)}, u32[]{:S(2)}) copy-start(bf16[256,2048]{1,0:T(8,128)(2,1)} %param.19) | copy-start | bytes 3145732
  463.2 206.5 %copy-start.32 = (bf16[256,4,128]{0,2,1:T(8,128)(2,1)}, bf16[256,4,128]{0,2,1:T(8,128)(2,1)S(1)}, u32[]{:S(2)}) copy-start(bf16[256,4,128]{0,2,1:T(8,128)(2,1)S(1)} %copy.113) | copy-start | bytes 786436
  466.8 316.9 %all-reduce.7.cloned.1.call-start = ((), (), s32[]{:S(2)}) async-start(), calls=%async_computation.6 | async-start | bytes 2097152 | tf_op jit(solution)/shard_map/psum | solution.py:167
  707.3 4.0 copy-start.9
  711.7 5.9 copy-start.63
  725.1 6.5 copy-start.29
  725.1 6.5 copy-start.31
  738.4 249.1 %all-gather.11.cloned.1.call-start = ((), (), s32[]{:S(2)}) async-start(), calls=%async_computation.7 | async-start | bytes 17301504 | tf_op jit(solution)/shard_map/all_gather | solution.py:12
  789.6 3.5 copy-start.42
  789.6 3.5 copy-start.62
  789.6 6.1 copy-start.60
  789.6 8.7 copy-start.34
  789.6 8.7 copy-start.50
  789.6 8.7 copy-start.56
  789.6 8.7 copy-start.52
  789.7 8.7 copy-start.58
  793.0 377.6 %all-reduce.9.cloned.1.call-start = ((), (), s32[]{:S(2)}) async-start(), calls=%async_computation.10 | async-start | bytes 4194304 | tf_op jit(solution)/shard_map/psum | solution.py:154
  798.4 7.0 copy-start.30
  805.3 5.6 copy-start.27
  810.9 7.0 slice-start
  811.0 7.0 slice-start.1
  811.0 7.6 copy-start.17
  818.6 4.1 copy-start.8
  1045.7 4.2 copy-start.5
  1048.2 3.3 copy-start.12
  1051.5 8.7 copy-start.35
  1060.2 6.8 copy-start.4
  1067.0 3.3 copy-start.11
  1070.5 17.4 %copy-start.25 = (bf16[256,4,128]{0,2,1:T(8,128)(2,1)}, bf16[256,4,128]{0,2,1:T(8,128)(2,1)S(1)}, u32[]{:S(2)}) copy-start(bf16[256,4,128]{0,2,1:T(8,128)(2,1)S(1)} %copy.138) | copy-start | bytes 786436
  1078.4 3.2 copy-start.20
  1083.1 4.8 copy-start.23
  1087.9 3.6 copy-start.22
  1087.9 3.6 copy-start.28
  1091.4 336.8 %reduce-scatter.9.cloned.1.call-start = ((), (), s32[]{:S(2)}) async-start(), calls=%async_computation.9 | async-start | bytes 25952256
  1148.6 3.3 copy-start.1
  1148.6 3.3 copy-start.44
  1148.7 3.3 copy-start.46
  1148.7 458.2 %reduce-scatter.7.cloned.1.call-start = ((), (), s32[]{:S(2)}) async-start(), calls=%async_computation.8 | async-start | bytes 8650752
  (11 other events, 18.2 us)
Sparse Core Ops, SparseCore 0:
  10.2 169.4 all-gather.4
  190.1 194.3 all-gather.6
  386.7 275.8 all-gather.8
  665.6 41.7 all-reduce.4
  738.5 45.0 all-reduce.6
  793.1 194.4 all-gather.10
  1091.6 57.5 all-reduce.8
  1151.7 276.5 reduce-scatter.8
  1430.8 176.0 reduce-scatter.6
where the time goes:
time: 1630 us; the launch traced here: 1620 us
  waiting for transfers between devices  1110 us (68%)
  local copies, waits for them, and re-layouts  201 us (12%)
  matrix products  149 us (9%)
  blocking collectives  83.9 us (5%)
  other arithmetic  59.9 us (4%)
    all_gather x4, waiting for transfers between devices, side_by_side(): whole = lax.all_gather(both, axis, axis=dim, tiled=True)  605 us
    unnamed x11, waiting for transfers between devices  420 us
    all_gather x1, blocking collectives, side_by_side(): whole = lax.all_gather(both, axis, axis=dim, tiled=True)  83.9 us
    unnamed x149, local copies, waits for them, and re-layouts  74.1 us
    psum x1, waiting for transfers between devices, local(): back_two = lax.psum(back_two.astype(jnp.bfloat16), 'tp').astype(jnp.float32)  45 us
    psum x1, waiting for transfers between devices, local(): lax.psum(attn_part.astype(jnp.bfloat16), 'tp').astype(jnp.float32)  37.7 us
  transfers between devices with their start and end apart: 9, of which 8 were waited for; matrix products, arithmetic and copies ran while one was open for 15% of the time, Pallas kernels for 0%

commit v1 on v0

v1 whole, which is shorter than its diff:
```python
import functools

import jax
import jax.numpy as jnp
from jax import lax
from jax.experimental import pallas as pl
from jax.experimental.pallas import tpu as pltpu
from jax.sharding import PartitionSpec as P

HEAD = 128
NY, NZL, NX = 4, 2, 4
BOTH = ("ctx", "tp")
QB = 256
KC = 512
LOG2E = 1.4426950408889634
VMEM_LIMIT = 56 * 1024 * 1024
F32, BF16 = jnp.float32, jnp.bfloat16


def ctx_index(y, zl, x):
    return (y * NZL + zl) * NX + x


XY_GROUPS = [
    [ctx_index(y, zl, x) for y in range(NY) for x in range(NX)] for zl in range(NZL)
]
X_GROUPS = [
    [ctx_index(y, zl, x) for x in range(NX)] for y in range(NY) for zl in range(NZL)
]


def flip(values, zl=0, zh=0, co=0):
    pairs = []
    for y in range(NY):
        for a in range(NZL):
            for x in range(NX):
                for t in range(4):
                    here = ctx_index(y, a, x) * 4 + t
                    there = ctx_index(y, a ^ zl, x) * 4 + (t ^ (2 * zh + co))
                    pairs.append((here, there))
    return lax.ppermute(values, BOTH, pairs)


def ring(values, dx=0, dy=0):
    pairs = [
        (ctx_index(y, a, x), ctx_index((y + dy) % NY, a, (x + dx) % NX))
        for y in range(NY)
        for a in range(NZL)
        for x in range(NX)
    ]
    return lax.ppermute(values, "ctx", pairs)


def turn(values, axis, bit):
    return jnp.where(bit == 1, jnp.flip(values, axis), values)


def norm(values):
    average = jnp.mean(values, axis=-1, keepdims=True)
    centred = values - average
    inverse = lax.rsqrt(jnp.mean(centred * centred, axis=-1, keepdims=True) + 1e-05)
    return centred * inverse, inverse


def norm_back(grad, normed, inverse):
    first = jnp.mean(grad, axis=-1, keepdims=True)
    second = jnp.mean(grad * normed, axis=-1, keepdims=True)
    return inverse * (grad - first - normed * second)


def column_sum(keep, send, work=()):
    work = iter(work)

    def meanwhile(values, *sent):
        job = next(work, None)
        return values if job is None else hold(values, job(sent))

    rows = keep.shape[0] // 4
    cut = rows // 2
    got = flip(send, co=1)
    half = keep.astype(F32) + got.astype(F32)
    own, far, near, both = (half[k * rows : (k + 1) * rows] for k in range(4))
    low, high = far[:cut].astype(BF16), far[cut:].astype(BF16)
    for_both, for_near = flip(low, zl=1), flip(high, zl=1, zh=1)
    near = meanwhile(near, low, high)
    near = jnp.concatenate([near[:cut], near[cut:] + for_near.astype(F32)], axis=0).astype(BF16)
    both = jnp.concatenate([both[:cut] + for_both.astype(F32), both[cut:]], axis=0).astype(BF16)
    from_near, from_both = flip(near, zl=1), flip(both, zl=1, zh=1)
    return meanwhile(own, near, both) + from_near.astype(F32) + from_both.astype(F32)


def column_gather(rows, work=()):
    work = iter(work)

    def meanwhile(values, *sent):
        job = next(work, None)
        return values if job is None else hold(values, job(sent))

    cut = rows.shape[0] // 2
    near, both = flip(rows, zl=1), flip(rows, zl=1, zh=1)
    low, high = meanwhile(both[:cut], rows), near[cut:]
    far_low, far_high = flip(low, zl=1), flip(high, zl=1, zh=1)
    far_low = meanwhile(far_low, low, high)
    half = [rows, far_low, far_high, near, both]
    return half + [flip(piece, co=1) for piece in half]


def ring_sum(parts, **step):
    forth, back = step, {k: -v for k, v in step.items()}
    ahead, behind = ring(parts[2][0], **forth), ring(parts[2][1], **back)
    from_back, from_forth = ring(parts[1][1], **forth), ring(parts[3][0], **back)
    low = parts[1][0].astype(F32) + ahead.astype(F32)
    high = parts[3][1].astype(F32) + behind.astype(F32)
    low, high = ring(low.astype(BF16), **forth), ring(high.astype(BF16), **back)
    return (
        parts[0][0].astype(F32) + low.astype(F32) + from_forth.astype(F32),
        parts[0][1].astype(F32) + from_back.astype(F32) + high.astype(F32),
    )


def ring_gather(rows, **step):
    forth, back = step, {k: -v for k, v in step.items()}
    cut = rows.shape[0] // 2
    before, after = ring(rows, **forth), ring(rows, **back)
    return rows, after, ring(before[:cut], **forth), ring(after[cut:], **back), before


def plane_gather(rows):
    half = rows.shape[1] // 2
    own = rows[:, :half], rows[:, half:]
    lines = [[ring(own[w], **{axis: -k}) for k in (1, 2, 3)] for w, axis in enumerate(("dx", "dy"))]
    by_x, by_y = (
        jnp.concatenate([hold(own[w], lines[1 - w][1])] + lines[w], axis=0) for w in range(2)
    )
    cut = by_x.shape[0] // 2
    x_before, x_after = ring(by_x, dy=1), ring(by_x, dy=-1)
    y_before, y_after = ring(by_y, dx=1), ring(by_y, dx=-1)
    x_low, x_high = ring(hold(x_before[:cut], y_after), dy=1), ring(x_after[cut:], dy=-1)
    y_low, y_high = ring(hold(y_before[:cut], x_after), dx=1), ring(y_after[cut:], dx=-1)
    return (by_x, x_after, x_low, x_high, x_before), (by_y, y_after, y_low, y_high, y_before)


def dot(left, right):
    return jnp.dot(left, right, preferred_element_type=F32)


def dot_nt(left, right):
    return lax.dot_general(left, right, (((1,), (1,)), ((), ())), preferred_element_type=F32)


def dot_tn(left, right):
    return lax.dot_general(left, right, (((0,), (0,)), ((), ())), preferred_element_type=F32)


def call(kernel, name, outs, scalars, arrays, after=(), scratch=(), flops=1, specs=None):
    head, tail = len(scalars) + len(arrays), len(after)
    vmem = pl.BlockSpec(memory_space=pltpu.VMEM)
    specs = specs or {}
    grid = {"grid": (1,)} if specs else {}

    def body(*refs):
        kernel(*refs[:head], *refs[head + tail :])

    return pl.pallas_call(
        body,
        **grid,
        out_shape=tuple(jax.ShapeDtypeStruct(shape, dtype) for shape, dtype in outs),
        in_specs=[pl.BlockSpec(memory_space=pltpu.SMEM)] * len(scalars)
        + [specs.get(k, vmem) for k in range(len(arrays))]
        + [pl.BlockSpec(memory_space=pl.ANY)] * tail,
        out_specs=(vmem,) * len(outs),
        scratch_shapes=list(scratch),
        compiler_params=pltpu.CompilerParams(vmem_limit_bytes=VMEM_LIMIT),
        cost_estimate=pl.CostEstimate(flops=flops, bytes_accessed=1, transcendentals=0),
        name=name,
    )(*[jnp.stack(s).astype(jnp.int32) for s in scalars], *arrays, *after)


def hold(values, token):
    return values + (token.reshape(-1)[0] * 0).astype(values.dtype)


def put_rows(to_ref, refs):
    row = 0
    for ref in refs:
        to_ref[row : row + ref.shape[0], :] = ref[...]
        row += ref.shape[0]


def enter_kernel(at, x_ref, dy_ref, a_ref, dy_out, own_ref):
    tile = own_ref.shape[0]
    lane = lax.broadcasted_iota(jnp.int32, (tile, HEAD), 1)
    for k in range(4):
        row = ((k // 2) ^ at[0]) * 2 + ((k % 2) ^ at[1])
        rows = pl.ds(pl.multiple_of(row * tile, tile), tile)
        x = x_ref[rows, :].astype(F32)
        values = [(norm(x)[0], a_ref), (dy_ref[rows, :].astype(F32), dy_out)]
        if k == 0:
            values.append((x, own_ref))
        for value, to_ref in values:
            for y in range(NY):
                for half in range(NX // 2):
                    pair = [
                        value[:, c : c + HEAD]
                        for c in [(y * NZL + z) * NX * HEAD // 2 + half * HEAD for z in range(2)]
                    ]
                    turned = [pltpu.roll(v, HEAD // 2, 1) for v in pair]
                    low = jnp.where(lane < HEAD // 2, pair[0], turned[1])
                    high = jnp.where(lane < HEAD // 2, turned[0], pair[1])
                    for n, v in enumerate((low, high)):
                        c = (y * NX + 2 * half + n) * HEAD
                        to_ref[k * tile : (k + 1) * tile, c : c + HEAD] = v.astype(BF16)


def enter(co, zh, x, dy):
    rows, width = x.shape
    outs = [((rows, width), BF16)] * 2 + [((rows // 4, width), BF16)]
    return call(enter_kernel, "enter", outs, [(co, zh)], [x, dy])


def each_piece(pairs):
    own, after, low, high, before = pairs
    for dy in range(NY):
        for x in range(NX):
            ref = (own, after, (low, high)[x // 2], before)[dy]
            for k in range(4):
                yield (dy * NX + x) * 4 + k, x % 2 if dy == 2 else x, k, ref


def sort_pairs(scalars, pairs, keys, values, tile):
    for slot, x, k, ref in each_piece(pairs):
        rows = pl.ds(pl.multiple_of(scalars[slot] * tile, tile), tile)
        keys[rows, :] = ref[x, 0, k * tile : (k + 1) * tile]
        values[rows, :] = ref[x, 1, k * tile : (k + 1) * tile]


def attend_kernel(
    scalars, q_ref, kv0, kv1, kv2, kv3, kv4, qblk, kblk, o_ref, full_ref, lse_ref, keys, values, queries, *, tile
):
    tiles = keys.shape[0] // tile
    per = QB // tile
    blocks = q_ref.shape[0] // per
    factor = HEAD**-0.5 * LOG2E
    sort_pairs(scalars, (kv0, kv1, kv2, kv3, kv4), keys, values, tile)

    def block(i, carry):
        for k in range(per):
            queries[k * tile : (k + 1) * tile, :] = q_ref[scalars[tiles + i * per + k]]
        q_own = queries[...]
        rows = pl.ds(pl.multiple_of(i * QB, QB), QB)

        def chunk(c, state, masked):
            top, total, acc = state
            where = pl.ds(pl.multiple_of(c * KC, KC), KC)
            s = dot_nt(q_own, keys[where, :])
            if masked:
                s = jnp.where(qblk[rows, :] >= kblk[:, where], s, -1e30)
            new = jnp.maximum(top, jnp.max(s, axis=-1, keepdims=True))
            p = jnp.exp2((s - new) * factor)
            shrink = jnp.exp2((top - new) * factor)
            total = total * shrink + jnp.sum(p, axis=-1, keepdims=True)
            acc = acc * shrink + dot(p.astype(BF16), values[where, :])
            return new, total, acc

        base = tiles + blocks * per
        state = (
            jnp.full((QB, 1), -1e30, F32),
            jnp.zeros((QB, 1), F32),
            jnp.zeros((QB, HEAD), F32),
        )
        first, last = scalars[base + i], scalars[base + blocks + i]
        state = lax.fori_loop(0, first, functools.partial(chunk, masked=False), state)
        top, total, acc = lax.fori_loop(first, last, functools.partial(chunk, masked=True), state)
        out = acc / total
        full_ref[rows, :] = out
        low = out.astype(BF16)
        for k in range(per):
            o_ref[scalars[tiles + i * per + k]] = low[k * tile : (k + 1) * tile]
        lse = top * factor + jnp.log2(total)
        lse_ref[i] = jnp.transpose(jnp.broadcast_to(lse, (QB, HEAD)))[:8]
        return carry

    lax.fori_loop(0, blocks, block, 0)


def attend(scalars, q, kv, qblk, kblk, after):
    tile = q.shape[1]
    count = q.shape[0] * tile
    length = kblk.shape[1]
    vmem = pl.BlockSpec(memory_space=pltpu.VMEM)
    kernel = functools.partial(attend_kernel, tile=tile)

    def body(*refs):
        kernel(*refs[:9], *refs[9 + len(after) :])

    return pl.pallas_call(
        body,
        out_shape=(
            jax.ShapeDtypeStruct(q.shape, BF16),
            jax.ShapeDtypeStruct((count, HEAD), F32),
            jax.ShapeDtypeStruct((count // QB, 8, QB), F32),
        ),
        in_specs=[pl.BlockSpec(memory_space=pltpu.SMEM)]
        + [vmem] * 8
        + [pl.BlockSpec(memory_space=pl.ANY)] * len(after),
        out_specs=(vmem,) * 3,
        scratch_shapes=[
            pltpu.VMEM((length, HEAD), BF16),
            pltpu.VMEM((length, HEAD), BF16),
            pltpu.VMEM((QB, HEAD), BF16),
        ],
        compiler_params=pltpu.CompilerParams(vmem_limit_bytes=VMEM_LIMIT),
        cost_estimate=pl.CostEstimate(
            flops=4 * count * length * HEAD, bytes_accessed=1 << 22, transcendentals=count * length
        ),
        name="attend",
    )(scalars, q, *kv, qblk, kblk, *after)


def attend_back_kernel(
    scalars,
    q_ref,
    kv0,
    kv1,
    kv2,
    kv3,
    kv4,
    do_ref,
    full_ref,
    lse_ref,
    qblk,
    kblk,
    dq_ref,
    own_ref,
    after_low,
    after_high,
    far_low,
    far_high,
    before_low,
    before_high,
    keys,
    values,
    queries,
    grads,
    dk,
    dv,
    *,
    tile,
):
    tiles = keys.shape[0] // tile
    per = QB // tile
    blocks = q_ref.shape[0] // per
    scale = HEAD**-0.5
    factor = scale * LOG2E
    sort_pairs(scalars, (kv0, kv1, kv2, kv3, kv4), keys, values, tile)
    dk[...] = jnp.zeros_like(dk)
    dv[...] = jnp.zeros_like(dv)

    def block(i, carry):
        for k in range(per):
            slot = scalars[tiles + i * per + k]
            queries[k * tile : (k + 1) * tile, :] = q_ref[slot]
            grads[k * tile : (k + 1) * tile, :] = do_ref[slot]
        q_own = queries[...]
        do_own = grads[...]
        rows = pl.ds(pl.multiple_of(i * QB, QB), QB)
        product = do_own.astype(F32) * full_ref[rows, :]
        delta = jnp.sum(jnp.transpose(product), axis=0, keepdims=True)
        lse = lse_ref[i][:1]
        q_blocks = qblk[i][:1]

        def chunk(c, acc, masked):
            where = pl.ds(pl.multiple_of(c * KC, KC), KC)
            k_own = keys[where, :]
            s = dot_nt(k_own, q_own)
            if masked:
                s = jnp.where(kblk[where, :] <= q_blocks, s, -1e30)
            p = jnp.exp2(s * factor - lse)
            dp = dot_nt(values[where, :], do_own)
            ds = (p * (dp - delta)).astype(BF16)
            dv[where, :] += dot(p.astype(BF16), do_own)
            dk[where, :] += dot(ds, q_own)
            return acc + dot_tn(ds, k_own)

        base = tiles + blocks * per
        first, last = scalars[base + i], scalars[base + blocks + i]
        acc = jnp.zeros((QB, HEAD), F32)
        acc = lax.fori_loop(0, first, functools.partial(chunk, masked=False), acc)
        acc = lax.fori_loop(first, last, functools.partial(chunk, masked=True), acc)
        low = (acc * scale).astype(BF16)
        for k in range(per):
            dq_ref[scalars[tiles + i * per + k]] = low[k * tile : (k + 1) * tile]
        return carry

    lax.fori_loop(0, blocks, block, 0)

    outs = ((own_ref, own_ref), (after_low, after_high), (far_low, far_high), (before_low, before_high))
    for slot in range(tiles):
        dy, x, k = slot // 16, slot // 4 % 4, slot % 4
        rows = pl.ds(pl.multiple_of(scalars[slot] * tile, tile), tile)
        ref, x = outs[dy][x // 2], x if dy == 0 else x % 2
        here = slice(k * tile, (k + 1) * tile)
        ref[x, 0, here] = (dk[rows, :] * scale).astype(BF16)
        ref[x, 1, here] = dv[rows, :].astype(BF16)


def attend_back(scalars, q, kv, do, full, lse, qblk, kblk):
    tile = q.shape[1]
    count = q.shape[0] * tile
    length = kblk.shape[0]
    vmem = pl.BlockSpec(memory_space=pltpu.VMEM)
    return pl.pallas_call(
        functools.partial(attend_back_kernel, tile=tile),
        out_shape=(
            jax.ShapeDtypeStruct(q.shape, BF16),
            jax.ShapeDtypeStruct(kv[0].shape, BF16),
        )
        + (jax.ShapeDtypeStruct(kv[2].shape, BF16),) * 6,
        in_specs=[pl.BlockSpec(memory_space=pltpu.SMEM)] + [vmem] * 11,
        out_specs=(vmem,) * 8,
        scratch_shapes=[
            pltpu.VMEM((length, HEAD), BF16),
            pltpu.VMEM((length, HEAD), BF16),
            pltpu.VMEM((QB, HEAD), BF16),
            pltpu.VMEM((QB, HEAD), BF16),
            pltpu.VMEM((length, HEAD), F32),
            pltpu.VMEM((length, HEAD), F32),
        ],
        compiler_params=pltpu.CompilerParams(vmem_limit_bytes=VMEM_LIMIT),
        cost_estimate=pl.CostEstimate(
            flops=10 * count * length * HEAD, bytes_accessed=1 << 23, transcendentals=count * length
        ),
        name="attend_back",
    )(scalars, q, *kv, do, full, lse, qblk, kblk)


def project_kernel(at, own_ref, near_ref, other_ref, *refs):
    parts, (cos_ref, sin_ref, q_ref, kv_ref, w_ref, a_ref) = refs[:10], refs[10:]
    half = own_ref.shape[0]
    put_rows(
        a_ref, [own_ref.at[: half // 2], near_ref, own_ref.at[half // 2 :], other_ref]
    )
    y, x = at[0], at[1]
    for way in range(2):
        own, after, low, high, before = parts[5 * way : 5 * way + 5]
        columns = slice(way * w_ref.shape[1] // 2, (way + 1) * w_ref.shape[1] // 2)
        for second in range(4):
            for first in range(4):
                ref = (own, after, (low, high)[first // 2], before)[second]
                row = (first % 2 if second == 2 else first) * HEAD
                dy, dx = (second, first) if way == 0 else (first, second)
                block = ((y + dy) % NY) * NX + (x + dx) % NX
                rows = pl.ds(pl.multiple_of(block * HEAD, HEAD), HEAD)
                w_ref[rows, columns] = ref[row : row + HEAD, :]
    cosine, sine = cos_ref[...], sin_ref[...]
    for part in range(3):
        product = dot(a_ref[...], w_ref[:, part * 2 * HEAD : (part + 1) * 2 * HEAD])
        for head in range(2):
            u = product[:, head * HEAD : (head + 1) * HEAD]
            if part < 2:
                u = u * cosine + pltpu.roll(u, HEAD // 2, 1) * sine
            u = u.astype(BF16)
            for ds in range(2):
                rows = u[ds * half : (ds + 1) * half]
                if part == 0:
                    q_ref[head * 2 + ds] = rows
                else:
                    kv_ref[head * 2 + ds, part - 1] = rows


def project(y, x, a, parts, cosine, sine):
    half, width = a[0].shape
    columns = 2 * parts[0].shape[1]
    return call(
        project_kernel,
        "project",
        [
            ((4, half, HEAD), BF16),
            ((4, 2, half, HEAD), BF16),
            ((width, columns), BF16),
        ],
        [(y, x)],
        [*a, *parts, cosine, sine],
        scratch=[pltpu.VMEM((2 * half, width), BF16)],
        flops=4 * half * width * 6 * HEAD,
    )


def output_kernel(o_ref, w_ref, keep_ref, send_ref):
    half = keep_ref.shape[0]
    o = jnp.concatenate([o_ref[0], o_ref[1]], axis=1)
    for c in range(0, keep_ref.shape[1], 512):
        part = dot_nt(o, w_ref[c : c + 512, :]).astype(BF16)
        keep_ref[:, c : c + 512] = part[:half]
        send_ref[:, c : c + 512] = part[half:]


def output(o_heads, attn_w):
    rows, width = o_heads.shape[1], attn_w.shape[0]
    spec = pl.BlockSpec((width, 2 * HEAD), lambda i: (0, 3))
    outs = [((rows // 2, width), BF16)] * 2
    flops = 4 * rows * width * HEAD
    return call(output_kernel, "output", outs, [], [o_heads, attn_w], flops=flops, specs={1: spec})


def mlp_kernel(*refs):
    b_parts, dy_parts = refs[:10], refs[10:13]
    w_ref, keep_ref, send_ref, dg_ref, du_ref, hidden_ref, b_ref, dy_ref = refs[13:]
    put_rows(b_ref, b_parts)
    half = dy_parts[0].shape[0]
    own, near, other = dy_parts
    put_rows(dy_ref, [own.at[: half // 2], near, own.at[half // 2 :], other])
    units = dg_ref.shape[1]
    for j in range(0, units, 256):
        here = slice(j, j + 256)
        gate = dot(b_ref[...], w_ref[:, j : j + 256])
        upper = dot(b_ref[...], w_ref[:, units + j : units + j + 256])
        grad = dot(dy_ref[...], w_ref[:, 2 * units + j : 2 * units + j + 256])
        sigmoid = 1.0 / (1.0 + jnp.exp(-gate))
        swish = gate * sigmoid
        hidden_ref[:, here] = (swish * upper).astype(BF16)
        du_ref[:, here] = (grad * swish).astype(BF16)
        dg_ref[:, here] = (grad * upper * sigmoid * (1.0 + gate * (1.0 - sigmoid))).astype(BF16)
    for c in range(0, keep_ref.shape[1], 512):
        part = dot_nt(dg_ref[...], w_ref[c : c + 512, :units])
        part = part + dot_nt(du_ref[...], w_ref[c : c + 512, units : 2 * units])
        part = part.astype(BF16)
        keep_ref[:, c : c + 512] = part[:half]
        send_ref[:, c : c + 512] = part[half:]


def mlp(b_parts, dy_parts, mlp_w):
    half, width = dy_parts[0].shape
    units = mlp_w.shape[1] // 3
    return call(
        mlp_kernel,
        "mlp",
        [((half, width), BF16)] * 2 + [((2 * half, units), BF16)] * 3,
        [],
        [*b_parts, *dy_parts, mlp_w],
        scratch=[pltpu.VMEM((2 * half, width), BF16)] * 2,
        flops=20 * half * width * units,
    )


def down_kernel(hidden_ref, w_ref, keep_ref, send_ref):
    half = keep_ref.shape[0]
    for c in range(0, keep_ref.shape[1], 512):
        part = dot_nt(hidden_ref[...], w_ref[c : c + 512, :]).astype(BF16)
        keep_ref[:, c : c + 512] = part[:half]
        send_ref[:, c : c + 512] = part[half:]


def down(hidden, mlp_w, after):
    (rows, units), width = hidden.shape, mlp_w.shape[0]
    spec = pl.BlockSpec((width, units), lambda i: (0, 2))
    outs = [((rows // 2, width), BF16)] * 2
    flops = 2 * rows * width * units
    return call(down_kernel, "down", outs, [], [hidden, mlp_w], after, flops=flops, specs={1: spec})


def grads_kernel(*refs, count, sources):
    lefts, (right_ref, out_ref, left_ref, turned) = refs[:count], refs[-4:]
    step = pl.program_id(0)

    def put():
        if sources is None:
            put_rows(left_ref, lefts)
        else:
            half = lefts[0].shape[0]
            own, near, other = lefts
            put_rows(left_ref, [own.at[: half // 2], near, own.at[half // 2 :], other])
        for r in range(0, turned.shape[0], 256):
            turned[r : r + 256, :] = jnp.transpose(left_ref[:, r : r + 256])

    pl.when(step == 0)(put)
    blocks = out_ref.shape[1]
    if len(right_ref.shape) == 3:
        right = jnp.concatenate([right_ref[k] for k in range(blocks)], axis=1)
    else:
        right = right_ref[...]
    for r in range(0, turned.shape[0], 256):
        product = dot(turned[r : r + 256, :], right).astype(BF16)
        for k in range(2):
            for c in range(blocks):
                out_ref[r // HEAD + k, c] = product[
                    k * HEAD : (k + 1) * HEAD, c * HEAD : (c + 1) * HEAD
                ]


def weight_grads(name, left, right, whole, first, total, after=()):
    width = left[0].shape[1]
    pairs = len(left) == 3
    tokens = sum(v.shape[0] for v in left)
    if right.ndim == 3:
        blocks, steps = right.shape[0], 1
        right_spec = pl.BlockSpec(right.shape, lambda i: (0, 0, 0))
    else:
        blocks = 4
        steps = right.shape[1] // (blocks * HEAD)
        right_spec = pl.BlockSpec((tokens, blocks * HEAD), lambda i: (0, i))
    vmem = pl.BlockSpec(memory_space=pltpu.VMEM)
    anywhere = pl.BlockSpec(memory_space=pl.ANY)
    before = list(after) + ([] if whole is None else [whole])
    kernel = functools.partial(
        grads_kernel, count=len(left), sources="pairs" if pairs else None
    )

    def body(*refs):
        kernel(*refs[: len(left) + 1], *refs[len(left) + 1 + len(before) :])

    return pl.pallas_call(
        body,
        grid=(steps,),
        out_shape=jax.ShapeDtypeStruct((width // HEAD, total, HEAD, HEAD), BF16),
        in_specs=[vmem] * len(left) + [right_spec] + [anywhere] * len(before),
        out_specs=pl.BlockSpec(
            (width // HEAD, blocks, HEAD, HEAD), lambda i: (0, first // blocks + i, 0, 0)
        ),
        scratch_shapes=[pltpu.VMEM((tokens, width), BF16), pltpu.VMEM((width, tokens), BF16)],
        input_output_aliases={} if whole is None else {len(left) + len(before): 0},
        compiler_params=pltpu.CompilerParams(vmem_limit_bytes=VMEM_LIMIT),
        cost_estimate=pl.CostEstimate(
            flops=tokens * width * blocks * steps * HEAD // 2, bytes_accessed=1, transcendentals=0
        ),
        name=name,
    )(*left, right, *before)


def outward_kernel(*refs):
    parts, (w_ref, do_ref, m_ref) = refs[:10], refs[10:]
    put_rows(m_ref, parts)
    part = dot(m_ref[...], w_ref[...]).astype(BF16)
    half = part.shape[0] // 2
    for head in range(2):
        for ds in range(2):
            do_ref[head * 2 + ds] = part[
                ds * half : (ds + 1) * half, head * HEAD : (head + 1) * HEAD
            ]


def outward(m_parts, attn_w):
    width = attn_w.shape[0]
    half = sum(v.shape[0] for v in m_parts) // 2
    spec = pl.BlockSpec((width, 2 * HEAD), lambda i: (0, 3))
    return call(
        outward_kernel,
        "outward",
        [((4, half, HEAD), BF16)],
        [],
        [*m_parts, attn_w],
        scratch=[pltpu.VMEM((2 * half, width), BF16)],
        flops=8 * half * width * HEAD,
        specs={len(m_parts): spec},
    )[0]


def back_kernel(dq_ref, dkv_ref, cos_ref, sin_ref, w_ref, keep_ref, send_ref, back_ref):
    half = dq_ref.shape[1]
    cosine, sine = cos_ref[...], sin_ref[...]
    for part in range(3):
        for head in range(2):
            for ds in range(2):
                unit = head * 2 + ds
                rows = slice(ds * half, (ds + 1) * half)
                if part == 0:
                    e = dq_ref[unit].astype(F32)
                else:
                    e = dkv_ref[unit, part - 1].astype(F32)
                if part < 2:
                    e = e * cosine[rows] - pltpu.roll(e, HEAD // 2, 1) * sine[rows]
                back_ref[part * 2 + head, rows] = e.astype(BF16)
    back = jnp.concatenate([back_ref[k] for k in range(6)], axis=1)
    for c in range(0, keep_ref.shape[1], 512):
        part = dot_nt(back, w_ref[c : c + 512, :]).astype(BF16)
        keep_ref[:, c : c + 512] = part[:half]
        send_ref[:, c : c + 512] = part[half:]


def backward(dq, dkv, cosine, sine, attn_w, after):
    half, width = dq.shape[1], attn_w.shape[0]
    spec = pl.BlockSpec((width, 6 * HEAD), lambda i: (0, 0))
    return call(
        back_kernel,
        "backward",
        [((half, width), BF16)] * 2 + [((6, 2 * half, HEAD), BF16)],
        [],
        [dq, dkv, cosine, sine, attn_w],
        after,
        flops=24 * half * width * HEAD,
        specs={4: spec},
    )


def total_kernel(at, terms_ref, keep_ref, send_ref):
    rows = keep_ref.shape[1]
    for c in range(keep_ref.shape[0]):
        total = terms_ref[0, c].astype(F32)
        for p in range(1, terms_ref.shape[0]):
            total = total + terms_ref[p, c].astype(F32)
        first, second = total[:rows], total[rows:]
        keep_ref[c] = jnp.where(at[0] == 0, first, second).astype(BF16)
        send_ref[c] = jnp.where(at[0] == 0, second, first).astype(BF16)


def total(zl, terms, after=()):
    outs = [((terms.shape[1], HEAD // 2, HEAD), BF16)] * 2
    return call(total_kernel, "total", outs, [(zl,)], [terms], after)


def place_kernel(at, keep_ref, got_ref, *outs):
    block = 0
    for out_ref in outs:
        half = out_ref.shape[1] // 2
        for c in range(0, half, HEAD):
            keep, got = keep_ref[block].astype(F32), got_ref[block].astype(F32)
            out_ref[:, c : c + HEAD] = jnp.where(at[0] == 0, keep, got)
            out_ref[:, half + c : half + c + HEAD] = jnp.where(at[0] == 0, got, keep)
            block += 1


def place(zl, sums, widths, after=()):
    keep, send = total(zl, sums, after)
    outs = [((HEAD // 2, 2 * w), F32) for w in widths]
    return call(place_kernel, "place", outs, [(zl,)], [keep, flip(send, zl=1)])


def finish_kernel(at, own_ref, far_ref, pair_ref, out_ref):
    tile = own_ref.shape[0]
    co, zh = at[0], at[1]
    lane = lax.broadcasted_iota(jnp.int32, (tile, HEAD), 1)
    for k in range(4):
        ref, start = ((own_ref, 0), (far_ref, 0), (pair_ref, 0), (pair_ref, tile))[k]
        at_row = ((k // 2) ^ co) * 2 + ((k % 2) ^ zh)
        rows = pl.ds(pl.multiple_of(at_row * tile, tile), tile)
        for y in range(NY):
            for half in range(NX // 2):
                pair = [
                    ref[start : start + tile, c : c + HEAD].astype(F32)
                    for c in ((y * NX + 2 * half) * HEAD, (y * NX + 2 * half + 1) * HEAD)
                ]
                turned = [pltpu.roll(v, HEAD // 2, 1) for v in pair]
                low = jnp.where(lane < HEAD // 2, pair[0], turned[1])
                high = jnp.where(lane < HEAD // 2, turned[0], pair[1])
                for zl, value in enumerate((low, high)):
                    column = (y * NZL + zl) * NX * HEAD // 2 + half * HEAD
                    out_ref[rows, column : column + HEAD] = value.astype(out_ref.dtype)


def finish(co, zh, own, dtype):
    far = flip(own, zh=1)
    pair = flip(jnp.concatenate([own, far], axis=0), co=1)
    vmem = pl.BlockSpec(memory_space=pltpu.VMEM)
    return pl.pallas_call(
        finish_kernel,
        out_shape=jax.ShapeDtypeStruct((4 * own.shape[0], own.shape[1]), dtype),
        in_specs=[pl.BlockSpec(memory_space=pltpu.SMEM)] + [vmem] * 3,
        out_specs=vmem,
        compiler_params=pltpu.CompilerParams(vmem_limit_bytes=VMEM_LIMIT),
        cost_estimate=pl.CostEstimate(flops=1, bytes_accessed=1, transcendentals=0),
        name="finish",
    )(jnp.stack([co, zh]).astype(jnp.int32), own, far, pair)


def local(
    tokens_in,
    w_query,
    w_key,
    w_value,
    w_output,
    w_gate,
    w_up,
    w_down,
    grad_out,
    block_ids,
    tile_order,
):
    own, width = tokens_in.shape
    seqs, length = block_ids.shape
    tile = length // tile_order.shape[1]
    wide = w_query.shape[1] // 2
    units = w_gate.shape[1] // 2
    piece = w_query.shape[0]
    ctx, tp = lax.axis_index("ctx"), lax.axis_index("tp")
    y, zl, x = ctx // (NZL * NX), (ctx // NX) % NZL, ctx % NX
    zh, co = tp // 2, tp % 2

    def pair_rows(arrays):
        def cut(array, which):
            half = array.shape[1] // 2
            return lax.dynamic_slice_in_dim(array, which * half, half, 1)

        kept = jnp.concatenate([cut(array, zl) for array in arrays], axis=1)
        sent = jnp.concatenate([cut(array, 1 - zl) for array in arrays], axis=1)
        return turn(jnp.stack([kept, flip(sent, zl=1)]), 0, zl).reshape(2 * piece, -1)

    first_own, grads, x_own = enter(co, zh, tokens_in, grad_out)
    pair = pair_rows((w_query, w_key, w_value, w_output))
    by_x, by_y = plane_gather(pair)
    near = flip(hold(first_own[: own // 2], pair), zl=1)
    first_low = [first_own, near, flip(near, co=1)]
    pair = pair_rows([hold(w, near) for w in (w_gate, w_up, w_down)])

    tiles = tile_order.reshape(seqs, NY, NZL, NX, 2)
    tiles = turn(turn(turn(tiles, 0, co), 2, zl), 4, zh)
    row_tiles = lax.dynamic_index_in_dim(tiles, y, 1, keepdims=False)
    own_tiles = lax.dynamic_index_in_dim(row_tiles, x, 2, keepdims=False).reshape(-1)
    positions = (own_tiles[:, None] * tile + jnp.arange(tile, dtype=jnp.int32)).reshape(-1)
    inverse = 10000.0 ** (-jnp.arange(0, HEAD, 2, dtype=F32) / HEAD)
    angles = positions.astype(F32)[:, None] * inverse[None, :]
    cosine = jnp.concatenate([jnp.cos(angles)] * 2, axis=-1)
    sine = jnp.concatenate([-jnp.sin(angles), jnp.sin(angles)], axis=-1)
    ds_own = x % 2
    unit_tiles = lax.dynamic_index_in_dim(tiles, ds_own, 0, keepdims=False)
    turns = (y + jnp.arange(NY, dtype=jnp.int32)) % NY
    key_tiles = jnp.swapaxes(jnp.take(unit_tiles, turns, axis=0), 1, 2).reshape(-1)
    query_tiles = lax.dynamic_index_in_dim(unit_tiles, y, 0, keepdims=False)
    query_tiles = jnp.swapaxes(query_tiles, 0, 1).reshape(-1)
    tile_count, query_count = key_tiles.shape[0], query_tiles.shape[0]
    rank = jnp.sum(query_tiles[None, :] < query_tiles[:, None], axis=1)
    places = jnp.arange(query_count, dtype=jnp.int32)
    order = jnp.sum(
        jnp.where(rank[None, :] == places[:, None], places[None, :], 0), axis=1
    ).astype(jnp.int32)
    sorted_tiles = jnp.sum(
        jnp.where(rank[None, :] == places[:, None], query_tiles[None, :], 0), axis=1
    )
    key_blocks = lax.dynamic_index_in_dim(block_ids, ds_own ^ co, 0, keepdims=False)
    query_blocks = jnp.take(key_blocks.reshape(tile_count, tile), sorted_tiles, axis=0).reshape(-1)
    by_block = query_blocks.reshape(-1, QB)
    sure = jnp.sum(key_blocks[None, :] <= by_block[:, :1], axis=1) // KC
    most = (jnp.sum(key_blocks[None, :] <= by_block[:, -1:], axis=1) + KC - 1) // KC
    scalars = jnp.concatenate([key_tiles, order, sure, most]).astype(jnp.int32)
    query_rows = jnp.broadcast_to(by_block[:, None, :], (by_block.shape[0], 8, QB))

    q_send, kv_send, attn_w = project(y, x, first_low, by_x + by_y, cosine, sine)
    half = own

    def across(values):
        return lax.all_to_all(values, "ctx", 0, 0, tiled=True, axis_index_groups=X_GROUPS)

    kv = ring_gather(across(kv_send), dy=1)
    mlp_w = lax.all_gather(
        hold(pair, kv[3]), "ctx", axis=0, tiled=True, axis_index_groups=XY_GROUPS
    )
    q = across(q_send).reshape(query_count, tile, HEAD)
    near = flip(hold(grads[: own // 2], q_send), zl=1)
    grad_all = [grads, near, flip(near, co=1)]
    o, o_full, lse = attend(
        scalars, q, kv, query_blocks[:, None], key_blocks[None, :], [grad_all[2]]
    )
    o_heads = across(o.reshape(NX, half, HEAD)).reshape(2, 2 * half, HEAD)
    attn_sum = column_sum(*output(o_heads, attn_w))

    x_own = x_own.astype(F32)
    dy_own = grads[:tile].astype(F32)
    middle = x_own + attn_sum
    normed_two, inverse_two = norm(middle)
    second_low = column_gather(normed_two.astype(BF16))
    keep, send, grad_gate, grad_up, hidden = mlp(second_low, grad_all, mlp_w)
    count, many = wide // HEAD, units // HEAD
    made = []

    def job(name, left, right):
        def run(after):
            whole = made[-1] if made else None
            made.append(
                weight_grads(name, left, right, whole, len(made) * many, 3 * many, after)
            )
            return made[-1]

        return run

    jobs = [
        job("grad_gate", second_low, grad_gate),
        job("grad_up", second_low, grad_up),
        job("grad_down", grad_all, hidden),
    ]
    back_two = column_sum(keep, send, jobs[:2])
    grad_middle = dy_own + norm_back(back_two, normed_two, inverse_two)
    parts = []

    def down_job(after):
        parts.extend(down(hidden, mlp_w, after))
        return parts[0]

    middle_low = column_gather(grad_middle.astype(BF16), [jobs[2], down_job])
    sums = lax.psum_scatter(
        made[-1], "ctx", scatter_dimension=0, tiled=True, axis_index_groups=XY_GROUPS
    )

    do_send = outward(middle_low, attn_w)
    do = across(do_send).reshape(query_count, tile, HEAD)
    dq, dkv, *others = attend_back(
        scalars, q, kv, do, o_full, lse, query_rows, key_blocks[:, None]
    )
    out_terms = weight_grads("grad_output", middle_low, o_heads, None, 0, count, [dq])
    out_terms = lax.all_to_all(
        out_terms, "ctx", 0, 0, tiled=True, axis_index_groups=XY_GROUPS
    )
    pairs = [(dkv[:2], dkv[2:])] + [tuple(others[2 * k : 2 * k + 2]) for k in range(3)]
    dkv = jnp.concatenate(ring_sum(pairs, dy=1), axis=0).astype(BF16)
    out_sum = column_sum(hold(parts[0], dq), hold(parts[1], dq))
    dq = across(dq.reshape(NX, half, HEAD))
    dkv = across(hold(dkv, out_terms))
    out_low = (middle + out_sum).astype(BF16)
    keep, send, back = backward(dq, dkv, cosine, sine, attn_w, [out_low])
    back_one = column_sum(keep, send)
    normed_own, inverse_own = norm(x_own)
    grad_own = grad_middle + norm_back(back_one, normed_own, inverse_own)
    grad_in = finish(co, zh, grad_own.astype(BF16), F32)
    tokens_out = finish(co, zh, out_low, BF16)
    terms = weight_grads("grad_qkv", first_low, back, None, 0, 3 * count)
    terms = lax.all_to_all(terms, "ctx", 0, 0, tiled=True, axis_index_groups=XY_GROUPS)
    mlp_out = place(zl, sums, (units,) * 3, [dq])
    return (
        tokens_out,
        grad_in,
        *place(zl, terms, (wide,) * 3, [grad_in, tokens_out, mlp_out[0]]),
        *place(zl, out_terms, (wide,), [dq]),
        *mlp_out,
    )


def solution(mesh):
    row, both = P("ctx", None), P("ctx", "tp")
    return jax.shard_map(
        local,
        mesh=mesh,
        in_specs=(row,) + (both,) * 7 + (row, P(), P()),
        out_specs=(row, row) + (both,) * 7,
        check_vma=False,
    )
```

time: 1630 us -> 511 us (0.31)
  waiting for transfers between devices: 1110 us -> 163 us
  local copies, waits for them, and re-layouts: 201 us -> 33.8 us
  matrix products: 149 us -> 0 us
  Pallas kernels: 0 us -> 127 us
  starting transfers between devices: 1.23 us -> 101 us
  blocking collectives: 83.9 us -> 14 us
  other arithmetic: 59.9 us -> 36.4 us
    all_gather x4 -> x1, waiting for transfers between devices: 605 us -> 0.02 us  [local(): lax.all_gather(hold(pair, kv[3]), 'ctx', axis=0, tiled=True, axis_index_g...]
    unnamed x11 -> x3, waiting for transfers between devices: 420 us -> 0.03 us
    dot_general x35 -> x0, matrix products: 149 us -> none  [the longest x2 15.7 us: local(): jnp.einsum('hqk,qhd->khd', score_low, queries_full, preferred_element_typ...]
    ppermute x0 -> x75, waiting for transfers between devices: none -> 136 us  [the longest x51 86.3 us: flip(): return lax.ppermute(values, BOTH, pairs)]
    pallas_call x0 -> x22, Pallas kernels: none -> 127 us  [the longest x13 62 us: call(): pl.pallas_call(body, **grid, out_shape=tuple((jax.ShapeDtypeStruct(shape,...]
    all_gather x1 -> x0, blocking collectives: 83.9 us -> none  [side_by_side(): whole = lax.all_gather(both, axis, axis=dim, tiled=True)]
    psum x3 -> x0, waiting for transfers between devices: 82.7 us -> none  [the longest x1 45 us: local(): back_two = lax.psum(back_two.astype(jnp.bfloat16), 'tp').astype(jnp.float32)]
    ppermute x0 -> x75, starting transfers between devices: none -> 73.8 us  [the longest x24 37.1 us: ring(): return lax.ppermute(values, 'ctx', pairs)]
  transfers between devices with their start and end apart: 9 -> 84, of which waited for: 8 -> 38; matrix products, arithmetic and copies ran while one was open for 15% -> 10% of each run, Pallas kernels for 0% -> 18%
where the time goes in v1:
time: 511 us; the launch traced here: 501 us
  waiting for transfers between devices  163 us (32%)
  Pallas kernels  127 us (25%)
  starting transfers between devices  101 us (20%)
  other arithmetic  36.4 us (7%)
  local copies, waits for them, and re-layouts  33.8 us (7%)
  between operations  25.1 us (5%)
  blocking collectives  14 us (3%)
    ppermute x51, waiting for transfers between devices, flip(): return lax.ppermute(values, BOTH, pairs)  86.3 us
    pallas_call x13, Pallas kernels, call(): pl.pallas_call(body, **grid, out_shape=tuple((jax.ShapeDtypeStruct(shape,...  62 us
    ppermute x24, waiting for transfers between devices, ring(): return lax.ppermute(values, 'ctx', pairs)  50 us
    ppermute x24, starting transfers between devices, ring(): return lax.ppermute(values, 'ctx', pairs)  37.1 us
    ppermute x51, starting transfers between devices, flip(): return lax.ppermute(values, BOTH, pairs)  36.7 us
    pallas_call x5, Pallas kernels, weight_grads(): pl.pallas_call(body, grid=(steps,), out_shape=jax.ShapeDtypeStruct((width...  27.4 us
    all_to_all x5, waiting for transfers between devices, across(): lax.all_to_all(values, 'ctx', 0, 0, tiled=True, axis_index_groups=X_GROUPS)  26.7 us
    all_to_all x5, starting transfers between devices, across(): lax.all_to_all(values, 'ctx', 0, 0, tiled=True, axis_index_groups=X_GROUPS)  19.1 us
  transfers between devices with their start and end apart: 84, of which 38 were waited for; matrix products, arithmetic and copies ran while one was open for 10% of the time, Pallas kernels for 18%

profile of v1, /device:TPU:0, one launch (start us, length us, event | category | flops | bytes accessed | tf_op | source)
XLA Modules:
  0.0 501.3 jit_solution(6627903086066678011)
XLA Ops:
  13.9 4.5 enter.1
  19.6 3.3 collective-permute-start.3
  23.6 2.6 collective-permute-start.9
  26.1 3.0 collective-permute-start.5
  36.5 2.2 collective-permute-done.6
  41.4 4.1 collective-permute-done.1.refs_2_.refs_1_
  52.7 2.6 collective-permute-start.16
  55.3 3.4 collective-permute-start.13
  60.4 2.3 collective-permute-done.13.refs_7_
  63.5 7.6 %project.1 = (bf16[4,256,128]{2,1,0:T(8,128)(2,1)}, bf16[4,2,256,128]{3,2,1,0:T(8,128)(2,1)}, bf16[2048,1024]{1,0:T(8,128)(2,1)}) custom-call(s32[2]{0:T(128)} %pad_add_fusion.2.refs_0_, bf16[256,2048]{1,0:T(8,128)(2,1)} %get-tuple-element.51.refs_1_.refs_0_, bf16[128,2048]{1,0:T(8,128)(2,1)} %copy-done.3, bf16[128,2048]{1,0:T(8,128)(2,1)} %copy-done.14, ...), custom_call_target="tpu_custom_call" | custom-call | flops 1610612736 | bytes 1 | tf_op jit(solution)/shard_map/project/pallas_call | solution.py:164
  71.0 3.5 all-to-all-start.1
  74.7 7.9 %all-to-all-done.1.refs_2_.kv0 = bf16[4,2,256,128]{3,2,1,0:T(8,128)(2,1)S(1)} async-done(((bf16[4,2,256,128]{3,2,1,0:T(8,128)(2,1)}), bf16[4,2,256,128]{3,2,1,0:T(8,128)(2,1)S(1)}, u32[]{:S(2)}, u32[]{:S(2)}) %all-to-all-start.1) | async-done | bytes 524320 | tf_op jit(solution)/shard_map/all_to_all | solution.py:840
  82.6 3.7 collective-permute-start.17
  86.8 7.8 %collective-permute-done.17.refs_3_.kv1 = bf16[4,2,256,128]{3,2,1,0:T(8,128)(2,1)S(1)} collective-permute-done((bf16[4,2,256,128]{3,2,1,0:T(8,128)(2,1)S(1)}, bf16[4,2,256,128]{3,2,1,0:T(8,128)(2,1)S(1)}, u32[]{:S(2)}, u32[]{:S(2)}) %collective-permute-start.17) | collective-permute-done | bytes 524320 | tf_op jit(solution)/shard_map/ppermute | solution.py:51
  94.6 3.8 collective-permute-start.20
  98.4 3.8 collective-permute-done.20.refs_5_.kv3
  111.9 8.6 %collective-permute-done.21.refs_11_.refs_1_ = bf16[128,2048]{1,0:T(8,128)(2,1)S(1)} collective-permute-done((bf16[128,2048]{1,0:T(8,128)(2,1)S(1)}, bf16[128,2048]{1,0:T(8,128)(2,1)S(1)}, u32[]{:S(2)}, u32[]{:S(2)}) %collective-permute-start.21) | collective-permute-done | bytes 524320 | tf_op jit(solution)/shard_map/ppermute | solution.py:41
  120.6 3.4 all-to-all-start
  124.1 4.1 collective-permute-done.18.refs_6_.kv4
  131.9 2.6 all-to-all-done
  134.5 6.4 %collective-permute-done.19.refs_4_.kv2 = bf16[2,2,256,128]{3,2,1,0:T(8,128)(2,1)S(1)} collective-permute-done((bf16[2,2,256,128]{3,2,1,0:T(8,128)(2,1)S(1)}, bf16[2,2,256,128]{3,2,1,0:T(8,128)(2,1)S(1)}, u32[]{:S(2)}, u32[]{:S(2)}) %collective-permute-start.19) | collective-permute-done | bytes 262176 | tf_op jit(solution)/shard_map/ppermute | solution.py:51
  141.6 14.7 %attend.1 = (bf16[16,64,128]{2,1,0:T(8,128)(2,1)}, f32[1024,128]{1,0:T(8,128)}, f32[4,8,256]{2,1,0:T(8,128)}) custom-call(s32[88]{0:T(128)} %pad_add_fusion.1.refs_0_.scalars, bf16[16,64,128]{2,1,0:T(8,128)(2,1)} %bitcast.99, bf16[4,2,256,128]{3,2,1,0:T(8,128)(2,1)} %copy-done.46, bf16[4,2,256,128]{3,2,1,0:T(8,128)(2,1)} %copy-done.61, ...), custom_call_target="tpu_custom_call" | custom-call | flops 2147483648 | bytes 4194304 | tf_op jit(solution)/shard_map/attend/pallas_call | solution.py:296
  156.3 14.0 %all_to_all.40 = bf16[4,256,128]{2,1,0:T(8,128)(2,1)} all-to-all(bf16[4,256,128]{2,1,0:T(8,128)(2,1)} %bitcast.102), channel_id=1, replica_groups={{0,4,8,12},{16,20,24,28},{32,36,40,44},{48,52,56,60},{64,68,72,76},{80,..., dimensions={0} | all-to-all | bytes 524288 | tf_op jit(solution)/shard_map/all_to_all | solution.py:840
  170.3 3.3 output.1
  173.6 2.9 collective-permute-done.23
  178.3 3.6 collective-permute-start.24
  181.9 3.8 collective-permute-done.24
  189.0 5.5 %collective-permute-done.25 = bf16[64,2048]{1,0:T(8,128)(2,1)S(1)} collective-permute-done((bf16[64,2048]{1,0:T(8,128)(2,1)S(1)}, bf16[64,2048]{1,0:T(8,128)(2,1)S(1)}, u32[]{:S(2)}, u32[]{:S(2)}) %collective-permute-start.25) | collective-permute-done | bytes 262176 | tf_op jit(solution)/shard_map/ppermute | solution.py:41
  198.5 6.2 %collective-permute-done.28.refs_4_ = bf16[64,2048]{1,0:T(8,128)(2,1)S(1)} collective-permute-done((bf16[64,2048]{1,0:T(8,128)(2,1)S(1)}, bf16[64,2048]{1,0:T(8,128)(2,1)S(1)}, u32[]{:S(2)}, u32[]{:S(2)}) %collective-permute-start.28) | collective-permute-done | bytes 262176 | tf_op jit(solution)/shard_map/ppermute | solution.py:41
  214.0 18.7 %mlp.1 = (bf16[256,2048]{1,0:T(8,128)(2,1)}, bf16[256,2048]{1,0:T(8,128)(2,1)}, bf16[512,1024]{1,0:T(8,128)(2,1)}, bf16[512,1024]{1,0:T(8,128)(2,1)}, bf16[512,1024]{1,0:T(8,128)(2,1)}) custom-call(bf16[64,2048]{1,0:T(8,128)(2,1)} %copy-done.9, bf16[32,2048]{1,0:T(8,128)(2,1)} %copy-done.37, bf16[32,2048]{1,0:T(8,128)(2,1)} %copy-done.38, ...), custom_call_target="tpu_custom_call" | custom-call | flops 10737418240 | bytes 1 | tf_op jit(solution)/shard_map/mlp/pallas_call | solution.py:164
  232.8 2.7 collective-permute-done.38
  239.7 6.2 %grad_gate.1.refs_13_ = bf16[16,24,128,128]{3,2,1,0:T(8,128)(2,1)} custom-call(bf16[64,2048]{1,0:T(8,128)(2,1)} %copy-done.9, bf16[32,2048]{1,0:T(8,128)(2,1)} %copy-done.37, bf16[32,2048]{1,0:T(8,128)(2,1)} %copy-done.38, bf16[64,2048]{1,0:T(8,128)(2,1)} %copy-done.18, bf16[64,2048]{1,0:T(8,128)(2,1)} %copy-done.17, bf16[64,2048]{1,0:T(8,128)(2,1)} %copy-done.24, ...), custom_call_target="tpu_custom_call" | custom-call | flops 536870912 | bytes 1 | tf_op jit(solution)/shard_map/grad_gate/pallas_call | solution.py:612
  254.4 6.2 %grad_up.1.refs_5_ = bf16[16,24,128,128]{3,2,1,0:T(8,128)(2,1)} custom-call(bf16[64,2048]{1,0:T(8,128)(2,1)} %copy-done.9, bf16[32,2048]{1,0:T(8,128)(2,1)} %copy-done.37, bf16[32,2048]{1,0:T(8,128)(2,1)} %copy-done.38, bf16[64,2048]{1,0:T(8,128)(2,1)} %copy-done.18, bf16[64,2048]{1,0:T(8,128)(2,1)} %copy-done.17, ...), custom_call_target="tpu_custom_call", output_to_operand_aliasing={{}: (13, {})} | custom-call | flops 536870912 | bytes 1 | tf_op jit(solution)/shard_map/grad_up/pallas_call | solution.py:612
  263.9 2.2 fusion.40
  266.1 6.2 %grad_down.1 = bf16[16,24,128,128]{3,2,1,0:T(8,128)(2,1)} custom-call(bf16[256,2048]{1,0:T(8,128)(2,1)} %get-tuple-element.54.refs_10_.refs_0_, bf16[128,2048]{1,0:T(8,128)(2,1)} %copy-done.35, bf16[128,2048]{1,0:T(8,128)(2,1)} %copy-done.36, bf16[512,1024]{1,0:T(8,128)(2,1)} %get-tuple-element.59.refs_3_.refs_0_, ...), custom_call_target="tpu_custom_call", output_to_operand_aliasing={{}: (5, {})} | custom-call | flops 536870912 | bytes 1 | tf_op jit(solution)/shard_map/grad_down/pallas_call | solution.py:612
  276.6 5.1 %collective-permute-done.43.refs_4_ = bf16[64,2048]{1,0:T(8,128)(2,1)S(1)} collective-permute-done((bf16[64,2048]{1,0:T(8,128)(2,1)S(1)}, bf16[64,2048]{1,0:T(8,128)(2,1)S(1)}, u32[]{:S(2)}, u32[]{:S(2)}) %collective-permute-start.43) | collective-permute-done | bytes 262176 | tf_op jit(solution)/shard_map/ppermute | solution.py:41
  283.5 6.2 %down.1 = (bf16[256,2048]{1,0:T(8,128)(2,1)}, bf16[256,2048]{1,0:T(8,128)(2,1)}) custom-call(bf16[512,1024]{1,0:T(8,128)(2,1)} %get-tuple-element.59.refs_3_.refs_0_, bf16[2048,3072]{1,0:T(8,128)(2,1)} %all-gather.2.cloned.1.call-done.refs_13_.refs_1_, bf16[32,2048]{1,0:T(8,128)(2,1)} %copy-done.42, bf16[32,2048]{1,0:T(8,128)(2,1)} %copy-done.41), custom_call_target="tpu_custom_call" | custom-call | flops 2147483648 | bytes 1 | tf_op jit(solution)/shard_map/down/pallas_call | solution.py:164
  296.3 3.5 outward.1
  299.7 3.6 all-to-all-start.3
  305.4 8.4 %all-to-all-done.3 = bf16[4,256,128]{2,1,0:T(8,128)(2,1)S(1)} async-done(((bf16[4,256,128]{2,1,0:T(8,128)(2,1)}), bf16[4,256,128]{2,1,0:T(8,128)(2,1)S(1)}, u32[]{:S(2)}, u32[]{:S(2)}) %all-to-all-start.3) | async-done | bytes 262176 | tf_op jit(solution)/shard_map/all_to_all | solution.py:840
  314.6 17.9 %attend_back.1 = (bf16[16,64,128]{2,1,0:T(8,128)(2,1)}, bf16[4,2,256,128]{3,2,1,0:T(8,128)(2,1)}, bf16[2,2,256,128]{3,2,1,0:T(8,128)(2,1)}, bf16[2,2,256,128]{3,...) custom-call(s32[88]{0:T(128)} %pad_add_fusion.1.refs_0_.scalars, ...), custom_call_target="tpu_custom_call" | custom-call | flops 5368709120 | bytes 8388608 | tf_op jit(solution)/shard_map/attend_back/pallas_call | solution.py:412
  335.6 3.4 grad_output.1
  339.0 4.4 all-to-all-start.5
  348.0 2.8 collective-permute-start.64
  354.3 16.5 %collective-permute-done.59 = bf16[2,2,256,128]{3,2,1,0:T(8,128)(2,1)S(1)} collective-permute-done((bf16[2,2,256,128]{3,2,1,0:T(8,128)(2,1)}, bf16[2,2,256,128]{3,2,1,0:T(8,128)(2,1)S(1)}, u32[]{:S(2)}, u32[]{:S(2)}) %collective-permute-start.59) | collective-permute-done | bytes 262176 | tf_op jit(solution)/shard_map/ppermute | solution.py:51
  372.4 3.8 collective-permute-done.55
  378.3 4.4 all-to-all-start.4
  384.6 3.6 collective-permute-done.60
  392.4 4.2 all-to-all-start.6
  398.5 7.8 %all-to-all-done.6.refs_1_ = bf16[4,2,256,128]{3,2,1,0:T(8,128)(2,1)} async-done(((bf16[4,2,256,128]{3,2,1,0:T(8,128)(2,1)}), bf16[4,2,256,128]{3,2,1,0:T(8,128)(2,1)}, u32[]{:S(2)}, u32[]{:S(2)}) %all-to-all-start.6) | async-done | bytes 524320 | tf_op jit(solution)/shard_map/all_to_all | solution.py:840
  406.3 5.7 %backward.1 = (bf16[256,2048]{1,0:T(8,128)(2,1)}, bf16[256,2048]{1,0:T(8,128)(2,1)}, bf16[6,512,128]{2,1,0:T(8,128)(2,1)}) custom-call(bf16[4,256,128]{2,1,0:T(8,128)(2,1)} %copy-done.11, bf16[4,2,256,128]{3,2,1,0:T(8,128)(2,1)} %all-to-all-done.6.refs_1_, f32[512,128]{1,0:T(8,128)} %get-tuple-element.167.refs_14_.refs_2_, ...), custom_call_target="tpu_custom_call" | custom-call | flops 1610612736 | bytes 1 | tf_op jit(solution)/shard_map/backward/pallas_call | solution.py:164
  412.0 2.9 collective-permute-done.65
  414.8 3.0 convert_add_fusion
  421.1 5.3 %grad_qkv.1 = bf16[16,6,128,128]{3,2,1,0:T(8,128)(2,1)} custom-call(bf16[256,2048]{1,0:T(8,128)(2,1)} %get-tuple-element.51.refs_1_.refs_0_, bf16[128,2048]{1,0:T(8,128)(2,1)} %copy-done.3, bf16[128,2048]{1,0:T(8,128)(2,1)} %copy-done.14, bf16[6,512,128]{2,1,0:T(8,128)(2,1)} %get-tuple-element.78.refs_3_), custom_call_target="tpu_custom_call" | custom-call | flops 402653184 | bytes 1 | tf_op jit(solution)/shard_map/grad_qkv/pallas_call | solution.py:612
  426.4 3.7 all-to-all-start.7
  436.7 5.0 %collective-permute-done.67 = bf16[64,2048]{1,0:T(8,128)(2,1)S(1)} collective-permute-done((bf16[64,2048]{1,0:T(8,128)(2,1)S(1)}, bf16[64,2048]{1,0:T(8,128)(2,1)S(1)}, u32[]{:S(2)}, u32[]{:S(2)}) %collective-permute-start.67) | collective-permute-done | bytes 262176 | tf_op jit(solution)/shard_map/ppermute | solution.py:41
  441.7 9.2 %collective-permute-done.69 = bf16[64,2048]{1,0:T(8,128)(2,1)S(1)} collective-permute-done((bf16[64,2048]{1,0:T(8,128)(2,1)S(1)}, bf16[64,2048]{1,0:T(8,128)(2,1)S(1)}, u32[]{:S(2)}, u32[]{:S(2)}) %collective-permute-start.69) | collective-permute-done | bytes 262176 | tf_op jit(solution)/shard_map/ppermute | solution.py:41
  452.5 7.0 %collective-permute-done.70.far_ref = bf16[64,2048]{1,0:T(8,128)(2,1)S(1)} collective-permute-done((bf16[64,2048]{1,0:T(8,128)(2,1)S(1)}, bf16[64,2048]{1,0:T(8,128)(2,1)S(1)}, u32[]{:S(2)}, u32[]{:S(2)}) %collective-permute-start.70) | collective-permute-done | bytes 262176 | tf_op jit(solution)/shard_map/ppermute | solution.py:41
  462.5 2.6 finish.2.refs_3_
  465.1 2.9 finish.3.refs_2_
  468.1 6.2 %collective-permute-done.72.refs_2_ = bf16[24,64,128]{2,1,0:T(8,128)(2,1)S(1)} collective-permute-done((bf16[24,64,128]{2,1,0:T(8,128)(2,1)}, bf16[24,64,128]{2,1,0:T(8,128)(2,1)S(1)}, u32[]{:S(2)}, u32[]{:S(2)}) %collective-permute-start.72) | collective-permute-done | bytes 393248 | tf_op jit(solution)/shard_map/ppermute | solution.py:41
  475.0 2.3 place.3
  479.3 3.0 total.4
  486.3 3.3 collective-permute-done.74.refs_2_
  (416 shorter events, 131.4 us)
Async XLA Ops:
  8.9 10.6 %collective-permute-start = (bf16[64,1024]{1,0:T(8,128)(2,1)S(1)}, bf16[64,1024]{1,0:T(8,128)(2,1)S(1)}, u32[]{:S(2)}, u32[]{:S(2)}) collective-permute-start(bf16[64,1024]{1,0:T(8,128)(2,1)S(1)} %pad_maximum_fusion.17), channel_id=1, source_target_pairs={{0,16},{1,17},{2,18},{3,19},{4,20},{5,21},{6,22},{7,23},{8,24},{9,... | collective-permute-start | bytes 393224 | tf_op jit(solution)/shard_map/ppermute | solution.py:41
  19.6 12.0 %collective-permute-start.3 = (bf16[128,512]{1,0:T(8,128)(2,1)S(1)}, bf16[128,512]{1,0:T(8,128)(2,1)S(1)}, u32[]{:S(2)}, u32[]{:S(2)}) collective-permute-start(bf16[128,512]{1,0:T(8,128)(2,1)S(1)} %get-tuple-element.146), channel_id=1, source_target_pairs={{0,64},{4,68},{8,72},{12,76},{16,80},{20,84},{24,88},{28,92},{32,9... | collective-permute-start | bytes 393224 | tf_op jit(solution)/shard_map/ppermute | solution.py:51
  22.9 12.3 %collective-permute-start.10 = (bf16[128,512]{1,0:T(8,128)(2,1)S(1)}, bf16[128,512]{1,0:T(8,128)(2,1)S(1)}, u32[]{:S(2)}, u32[]{:S(2)}) collective-permute-start(bf16[128,512]{1,0:T(8,128)(2,1)S(1)} %get-tuple-element.146), channel_id=1, source_target_pairs={{0,32},{4,36},{8,40},{12,44},{16,48},{20,52},{24,56},{28,60},{32,6... | collective-permute-start | bytes 393224 | tf_op jit(solution)/shard_map/ppermute | solution.py:51
  23.6 11.7 %collective-permute-start.9 = (bf16[128,512]{1,0:T(8,128)(2,1)S(1)}, bf16[128,512]{1,0:T(8,128)(2,1)S(1)}, u32[]{:S(2)}, u32[]{:S(2)}) collective-permute-start(bf16[128,512]{1,0:T(8,128)(2,1)S(1)} %get-tuple-element.146), channel_id=1, source_target_pairs={{0,96},{4,100},{8,104},{12,108},{16,112},{20,116},{24,120},{28,124... | collective-permute-start | bytes 393224 | tf_op jit(solution)/shard_map/ppermute | solution.py:51
  26.1 7.6 %collective-permute-start.5 = (bf16[128,512]{1,0:T(8,128)(2,1)S(1)}, bf16[128,512]{1,0:T(8,128)(2,1)S(1)}, u32[]{:S(2)}, u32[]{:S(2)}) collective-permute-start(bf16[128,512]{1,0:T(8,128)(2,1)S(1)} %get-tuple-element.147), channel_id=1, source_target_pairs={{0,8},{4,12},{8,0},{12,4},{16,24},{20,28},{24,16},{28,20},{32,40},... | collective-permute-start | bytes 393224 | tf_op jit(solution)/shard_map/ppermute | solution.py:51
  29.2 7.4 %collective-permute-start.4 = (bf16[128,512]{1,0:T(8,128)(2,1)S(1)}, bf16[128,512]{1,0:T(8,128)(2,1)S(1)}, u32[]{:S(2)}, u32[]{:S(2)}) collective-permute-start(bf16[128,512]{1,0:T(8,128)(2,1)S(1)} %get-tuple-element.147), channel_id=1, source_target_pairs={{0,12},{4,0},{8,4},{12,8},{16,28},{20,16},{24,20},{28,24},{32,44},... | collective-permute-start | bytes 393224 | tf_op jit(solution)/shard_map/ppermute | solution.py:51
  33.8 11.8 %collective-permute-start.1 = (bf16[128,2048]{1,0:T(8,128)(2,1)S(1)}, bf16[128,2048]{1,0:T(8,128)(2,1)S(1)}, u32[]{:S(2)}, u32[]{:S(2)}) collective-permute-start(bf16[128,2048]{1,0:T(8,128)(2,1)S(1)} %slice_add_fusion.6), channel_id=1, source_target_pairs={{0,16},{1,17},{2,18},{3,19},{4,20},{5,21},{6,22},{7,23},{8,24},{9,... | collective-permute-start | bytes 1572872 | tf_op jit(solution)/shard_map/ppermute | solution.py:41
  35.3 14.9 %collective-permute-start.14 = (bf16[512,512]{1,0:T(8,128)(2,1)S(1)}, bf16[512,512]{1,0:T(8,128)(2,1)S(1)}, u32[]{:S(2)}, u32[]{:S(2)}) collective-permute-start(bf16[512,512]{1,0:T(8,128)(2,1)S(1)} %pad_maximum_fusion.2.refs_9_), channel_id=1, source_target_pairs={{0,4},{4,8},{8,12},{12,0},{16,20},{20,24},{24,28},{28,16},{32,36},... | collective-permute-start | bytes 1572872 | tf_op jit(solution)/shard_map/ppermute | solution.py:51
  38.7 10.0 %collective-permute-start.7 = (bf16[512,512]{1,0:T(8,128)(2,1)S(1)}, bf16[512,512]{1,0:T(8,128)(2,1)S(1)}, u32[]{:S(2)}, u32[]{:S(2)}) collective-permute-start(bf16[512,512]{1,0:T(8,128)(2,1)S(1)} %pad_maximum_fusion.1.refs_4_), channel_id=1, source_target_pairs={{0,96},{4,100},{8,104},{12,108},{16,112},{20,116},{24,120},{28,124... | collective-permute-start | bytes 1572872 | tf_op jit(solution)/shard_map/ppermute | solution.py:51
  39.4 11.7 %collective-permute-start.11 = (bf16[512,512]{1,0:T(8,128)(2,1)S(1)}, bf16[512,512]{1,0:T(8,128)(2,1)S(1)}, u32[]{:S(2)}, u32[]{:S(2)}) collective-permute-start(bf16[512,512]{1,0:T(8,128)(2,1)S(1)} %pad_maximum_fusion.2.refs_9_), channel_id=1, source_target_pairs={{0,12},{4,0},{8,4},{12,8},{16,28},{20,16},{24,20},{28,24},{32,44},... | collective-permute-start | bytes 1572872 | tf_op jit(solution)/shard_map/ppermute | solution.py:51
  39.4 13.1 %collective-permute-start.8 = (bf16[512,512]{1,0:T(8,128)(2,1)S(1)}, bf16[512,512]{1,0:T(8,128)(2,1)S(1)}, u32[]{:S(2)}, u32[]{:S(2)}) collective-permute-start(bf16[512,512]{1,0:T(8,128)(2,1)S(1)} %pad_maximum_fusion.1.refs_4_), channel_id=1, source_target_pairs={{0,32},{4,36},{8,40},{12,44},{16,48},{20,52},{24,56},{28,60},{32,6... | collective-permute-start | bytes 1572872 | tf_op jit(solution)/shard_map/ppermute | solution.py:51
  46.9 15.7 %collective-permute-start.2 = (bf16[128,2048]{1,0:T(8,128)(2,1)S(1)}, bf16[128,2048]{1,0:T(8,128)(2,1)S(1)}, u32[]{:S(2)}, u32[]{:S(2)}) collective-permute-start(bf16[128,2048]{1,0:T(8,128)(2,1)S(1)} %collective-permute-done.1.refs_2_.refs_1_), channel_id=1, source_target_pairs={{0,1},{1,0},{2,3},{3,2},{4,5},{5,4},{6,7},{7,6},{8,9},{9,8},{10,11... | collective-permute-start | bytes 1572872 | tf_op jit(solution)/shard_map/ppermute | solution.py:41
  50.2 8.5 %collective-permute-start.15 = (bf16[256,512]{1,0:T(8,128)(2,1)S(1)}, bf16[256,512]{1,0:T(8,128)(2,1)S(1)}, u32[]{:S(2)}, u32[]{:S(2)}) collective-permute-start(bf16[256,512]{1,0:T(8,128)(2,1)S(1)} %slice_add_fusion.15), channel_id=1, source_target_pairs={{0,4},{4,8},{8,12},{12,0},{16,20},{20,24},{24,28},{28,16},{32,36},... | collective-permute-start | bytes 786440 | tf_op jit(solution)/shard_map/ppermute | solution.py:51
  52.6 7.8 %collective-permute-start.12 = (bf16[256,512]{1,0:T(8,128)(2,1)S(1)}, bf16[256,512]{1,0:T(8,128)(2,1)S(1)}, u32[]{:S(2)}, u32[]{:S(2)}) collective-permute-start(bf16[256,512]{1,0:T(8,128)(2,1)S(1)} %slice_add_fusion.16), channel_id=1, source_target_pairs={{0,32},{4,36},{8,40},{12,44},{16,48},{20,52},{24,56},{28,60},{32,6... | collective-permute-start | bytes 786440 | tf_op jit(solution)/shard_map/ppermute | solution.py:51
  52.7 7.7 %collective-permute-start.16 = (bf16[256,512]{1,0:T(8,128)(2,1)S(1)}, bf16[256,512]{1,0:T(8,128)(2,1)S(1)}, u32[]{:S(2)}, u32[]{:S(2)}) collective-permute-start(bf16[256,512]{1,0:T(8,128)(2,1)S(1)} %slice.316), channel_id=1, source_target_pairs={{0,12},{4,0},{8,4},{12,8},{16,28},{20,16},{24,20},{28,24},{32,44},... | collective-permute-start | bytes 786440 | tf_op jit(solution)/shard_map/ppermute | solution.py:51
  55.3 7.3 %collective-permute-start.13 = (bf16[256,512]{1,0:T(8,128)(2,1)S(1)}, bf16[256,512]{1,0:T(8,128)(2,1)S(1)}, u32[]{:S(2)}, u32[]{:S(2)}) collective-permute-start(bf16[256,512]{1,0:T(8,128)(2,1)S(1)} %slice.313), channel_id=1, source_target_pairs={{0,96},{4,100},{8,104},{12,108},{16,112},{20,116},{24,120},{28,124... | collective-permute-start | bytes 786440 | tf_op jit(solution)/shard_map/ppermute | solution.py:51
  71.0 11.5 %all-to-all-start.1 = ((bf16[4,2,256,128]{3,2,1,0:T(8,128)(2,1)}), bf16[4,2,256,128]{3,2,1,0:T(8,128)(2,1)S(1)}, u32[]{:S(2)}, u32[]{:S(2)}) async-start(bf16[4,2,256,128]{3,2,1,0:T(8,128)(2,1)} %get-tuple-element.53), calls=%async_computation.1 | async-start | bytes 1048576 | tf_op jit(solution)/shard_map/all_to_all | solution.py:840
  74.5 138.7 %all-gather.2.cloned.1.call-start = ((), (), s32[]{:S(2)}) async-start(), calls=%async_computation.9 | async-start | bytes 13369344 | tf_op jit(solution)/shard_map/all_gather | solution.py:843
  82.6 12.0 %collective-permute-start.17 = (bf16[4,2,256,128]{3,2,1,0:T(8,128)(2,1)S(1)}, bf16[4,2,256,128]{3,2,1,0:T(8,128)(2,1)S(1)}, u32[]{:S(2)}, u32[]{:S(2)}) collective-permute-start(bf16[4,2,256,128]{3,2,1,0:T(8,128)(2,1)S(1)} %all-to-all-done.1.refs_2_.kv0), channel_id=1, source_target_pairs={{0,96},{4,100},{8,104},{12,108},{16,112},{20,116},{24,120},{28,124... | collective-permute-start | bytes 1572872 | tf_op jit(solution)/shard_map/ppermute | solution.py:51
  86.3 12.1 %collective-permute-start.37 = (bf16[64,3072]{1,0:T(8,128)(2,1)S(1)}, bf16[64,3072]{1,0:T(8,128)(2,1)S(1)}, u32[]{:S(2)}, u32[]{:S(2)}) collective-permute-start(bf16[64,3072]{1,0:T(8,128)(2,1)S(1)} %pad_maximum_fusion.5), channel_id=1, source_target_pairs={{0,16},{1,17},{2,18},{3,19},{4,20},{5,21},{6,22},{7,23},{8,24},{9,... | collective-permute-start | bytes 1179656 | tf_op jit(solution)/shard_map/ppermute | solution.py:41
  94.6 7.7 %collective-permute-start.20 = (bf16[2,2,256,128]{3,2,1,0:T(8,128)(2,1)S(1)}, bf16[2,2,256,128]{3,2,1,0:T(8,128)(2,1)S(1)}, u32[]{:S(2)}, u32[]{:S(2)}) collective-permute-start(bf16[2,2,256,128]{3,2,1,0:T(8,128)(2,1)S(1)} %slice.318), channel_id=1, source_target_pairs={{0,96},{4,100},{8,104},{12,108},{16,112},{20,116},{24,120},{28,124... | collective-permute-start | bytes 786440 | tf_op jit(solution)/shard_map/ppermute | solution.py:51
  111.3 9.3 %collective-permute-start.21 = (bf16[128,2048]{1,0:T(8,128)(2,1)S(1)}, bf16[128,2048]{1,0:T(8,128)(2,1)S(1)}, u32[]{:S(2)}, u32[]{:S(2)}) collective-permute-start(bf16[128,2048]{1,0:T(8,128)(2,1)S(1)} %slice_add_fusion.5), channel_id=1, source_target_pairs={{0,16},{1,17},{2,18},{3,19},{4,20},{5,21},{6,22},{7,23},{8,24},{9,... | collective-permute-start | bytes 1572872 | tf_op jit(solution)/shard_map/ppermute | solution.py:41
  111.7 16.5 %collective-permute-start.18 = (bf16[4,2,256,128]{3,2,1,0:T(8,128)(2,1)S(1)}, bf16[4,2,256,128]{3,2,1,0:T(8,128)(2,1)S(1)}, u32[]{:S(2)}, u32[]{:S(2)}) collective-permute-start(bf16[4,2,256,128]{3,2,1,0:T(8,128)(2,1)S(1)} %all-to-all-done.1.refs_2_.kv0), channel_id=1, source_target_pairs={{0,32},{4,36},{8,40},{12,44},{16,48},{20,52},{24,56},{28,60},{32,6... | collective-permute-start | bytes 1572872 | tf_op jit(solution)/shard_map/ppermute | solution.py:51
  120.5 13.9 %collective-permute-start.22 = (bf16[128,2048]{1,0:T(8,128)(2,1)S(1)}, bf16[128,2048]{1,0:T(8,128)(2,1)S(1)}, u32[]{:S(2)}, u32[]{:S(2)}) collective-permute-start(bf16[128,2048]{1,0:T(8,128)(2,1)S(1)} %collective-permute-done.21.refs_11_.refs_1_), channel_id=1, source_target_pairs={{0,1},{1,0},{2,3},{3,2},{4,5},{5,4},{6,7},{7,6},{8,9},{9,8},{10,11... | collective-permute-start | bytes 1572872 | tf_op jit(solution)/shard_map/ppermute | solution.py:41
  120.6 13.9 %all-to-all-start = ((bf16[4,256,128]{2,1,0:T(8,128)(2,1)}), bf16[4,256,128]{2,1,0:T(8,128)(2,1)S(1)}, u32[]{:S(2)}, u32[]{:S(2)}) async-start(bf16[4,256,128]{2,1,0:T(8,128)(2,1)} %get-tuple-element.52), calls=%async_computation | async-start | bytes 524288 | tf_op jit(solution)/shard_map/all_to_all | solution.py:840
  124.0 336.3 %reduce-scatter.4.cloned.1.call-start = ((), (), s32[]{:S(2)}) async-start(), calls=%async_computation.10 | async-start | bytes 13369344
  128.2 12.7 %collective-permute-start.19 = (bf16[2,2,256,128]{3,2,1,0:T(8,128)(2,1)S(1)}, bf16[2,2,256,128]{3,2,1,0:T(8,128)(2,1)S(1)}, u32[]{:S(2)}, u32[]{:S(2)}) collective-permute-start(bf16[2,2,256,128]{3,2,1,0:T(8,128)(2,1)S(1)} %slice.317), channel_id=1, source_target_pairs={{0,32},{4,36},{8,40},{12,44},{16,48},{20,52},{24,56},{28,60},{32,6... | collective-permute-start | bytes 786440 | tf_op jit(solution)/shard_map/ppermute | solution.py:51
  178.3 7.4 %collective-permute-start.24 = (bf16[32,2048]{1,0:T(8,128)(2,1)S(1)}, bf16[32,2048]{1,0:T(8,128)(2,1)S(1)}, u32[]{:S(2)}, u32[]{:S(2)}) collective-permute-start(bf16[32,2048]{1,0:T(8,128)(2,1)S(1)} %get-tuple-element.134), channel_id=1, source_target_pairs={{0,18},{1,19},{2,16},{3,17},{4,22},{5,23},{6,20},{7,21},{8,26},{9,... | collective-permute-start | bytes 393224 | tf_op jit(solution)/shard_map/ppermute | solution.py:41
  187.2 7.4 %collective-permute-start.25 = (bf16[64,2048]{1,0:T(8,128)(2,1)S(1)}, bf16[64,2048]{1,0:T(8,128)(2,1)S(1)}, u32[]{:S(2)}, u32[]{:S(2)}) collective-permute-start(bf16[64,2048]{1,0:T(8,128)(2,1)S(1)} %pad_maximum_fusion.9), channel_id=1, source_target_pairs={{0,16},{1,17},{2,18},{3,19},{4,20},{5,21},{6,22},{7,23},{8,24},{9,... | collective-permute-start | bytes 786440 | tf_op jit(solution)/shard_map/ppermute | solution.py:41
  187.6 8.6 %collective-permute-start.27 = (bf16[64,2048]{1,0:T(8,128)(2,1)S(1)}, bf16[64,2048]{1,0:T(8,128)(2,1)S(1)}, u32[]{:S(2)}, u32[]{:S(2)}) collective-permute-start(bf16[64,2048]{1,0:T(8,128)(2,1)S(1)} %pad_maximum_fusion.10), channel_id=1, source_target_pairs={{0,18},{1,19},{2,16},{3,17},{4,22},{5,23},{6,20},{7,21},{8,26},{9,... | collective-permute-start | bytes 786440 | tf_op jit(solution)/shard_map/ppermute | solution.py:41
  196.9 7.8 %collective-permute-start.28 = (bf16[64,2048]{1,0:T(8,128)(2,1)S(1)}, bf16[64,2048]{1,0:T(8,128)(2,1)S(1)}, u32[]{:S(2)}, u32[]{:S(2)}) collective-permute-start(bf16[64,2048]{1,0:T(8,128)(2,1)S(1)} %fusion.18.refs_0_), channel_id=1, source_target_pairs={{0,18},{1,19},{2,16},{3,17},{4,22},{5,23},{6,20},{7,21},{8,26},{9,... | collective-permute-start | bytes 786440 | tf_op jit(solution)/shard_map/ppermute | solution.py:41
  198.5 13.3 %collective-permute-start.32 = (bf16[64,2048]{1,0:T(8,128)(2,1)S(1)}, bf16[64,2048]{1,0:T(8,128)(2,1)S(1)}, u32[]{:S(2)}, u32[]{:S(2)}) collective-permute-start(bf16[64,2048]{1,0:T(8,128)(2,1)S(1)} %fusion.18.refs_0_), channel_id=1, source_target_pairs={{0,1},{1,0},{2,3},{3,2},{4,5},{5,4},{6,7},{7,6},{8,9},{9,8},{10,11... | collective-permute-start | bytes 786440 | tf_op jit(solution)/shard_map/ppermute | solution.py:41
  237.9 9.8 %collective-permute-start.39 = (bf16[32,2048]{1,0:T(8,128)(2,1)}, bf16[32,2048]{1,0:T(8,128)(2,1)}, u32[]{:S(2)}, u32[]{:S(2)}) collective-permute-start(bf16[32,2048]{1,0:T(8,128)(2,1)} %get-tuple-element.128.refs_12_), channel_id=1, source_target_pairs={{0,18},{1,19},{2,16},{3,17},{4,22},{5,23},{6,20},{7,21},{8,26},{9,... | collective-permute-start | bytes 393224 | tf_op jit(solution)/shard_map/ppermute | solution.py:41
  239.4 11.3 %collective-permute-start.40 = (bf16[32,2048]{1,0:T(8,128)(2,1)}, bf16[32,2048]{1,0:T(8,128)(2,1)}, u32[]{:S(2)}, u32[]{:S(2)}) collective-permute-start(bf16[32,2048]{1,0:T(8,128)(2,1)} %get-tuple-element.130.refs_11_), channel_id=1, source_target_pairs={{0,16},{1,17},{2,18},{3,19},{4,20},{5,21},{6,22},{7,23},{8,24},{9,... | collective-permute-start | bytes 393224 | tf_op jit(solution)/shard_map/ppermute | solution.py:41
  248.7 13.7 %collective-permute-start.41 = (bf16[64,2048]{1,0:T(8,128)(2,1)S(1)}, bf16[64,2048]{1,0:T(8,128)(2,1)}, u32[]{:S(2)}, u32[]{:S(2)}) collective-permute-start(bf16[64,2048]{1,0:T(8,128)(2,1)S(1)} %pad_maximum_fusion.11.refs_11_), channel_id=1, source_target_pairs={{0,16},{1,17},{2,18},{3,19},{4,20},{5,21},{6,22},{7,23},{8,24},{9,... | collective-permute-start | bytes 786440 | tf_op jit(solution)/shard_map/ppermute | solution.py:41
  252.5 9.9 %collective-permute-start.42 = (bf16[64,2048]{1,0:T(8,128)(2,1)S(1)}, bf16[64,2048]{1,0:T(8,128)(2,1)}, u32[]{:S(2)}, u32[]{:S(2)}) collective-permute-start(bf16[64,2048]{1,0:T(8,128)(2,1)S(1)} %pad_maximum_fusion.12.refs_12_), channel_id=1, source_target_pairs={{0,18},{1,19},{2,16},{3,17},{4,22},{5,23},{6,20},{7,21},{8,26},{9,... | collective-permute-start | bytes 786440 | tf_op jit(solution)/shard_map/ppermute | solution.py:41
  273.2 8.4 %collective-permute-start.43 = (bf16[64,2048]{1,0:T(8,128)(2,1)S(1)}, bf16[64,2048]{1,0:T(8,128)(2,1)S(1)}, u32[]{:S(2)}, u32[]{:S(2)}) collective-permute-start(bf16[64,2048]{1,0:T(8,128)(2,1)S(1)} %copy-done.4), channel_id=1, source_target_pairs={{0,18},{1,19},{2,16},{3,17},{4,22},{5,23},{6,20},{7,21},{8,26},{9,... | collective-permute-start | bytes 786440 | tf_op jit(solution)/shard_map/ppermute | solution.py:41
  274.7 18.9 %collective-permute-start.47 = (bf16[64,2048]{1,0:T(8,128)(2,1)S(1)}, bf16[64,2048]{1,0:T(8,128)(2,1)S(1)}, u32[]{:S(2)}, u32[]{:S(2)}) collective-permute-start(bf16[64,2048]{1,0:T(8,128)(2,1)S(1)} %copy-done.4), channel_id=1, source_target_pairs={{0,1},{1,0},{2,3},{3,2},{4,5},{5,4},{6,7},{7,6},{8,9},{9,8},{10,11... | collective-permute-start | bytes 786440 | tf_op jit(solution)/shard_map/ppermute | solution.py:41
  281.7 11.3 %collective-permute-start.45 = (bf16[32,2048]{1,0:T(8,128)(2,1)S(1)}, bf16[32,2048]{1,0:T(8,128)(2,1)S(1)}, u32[]{:S(2)}, u32[]{:S(2)}) collective-permute-start(bf16[32,2048]{1,0:T(8,128)(2,1)S(1)} %slice_add_fusion.17.refs_2_), channel_id=1, source_target_pairs={{0,16},{1,17},{2,18},{3,19},{4,20},{5,21},{6,22},{7,23},{8,24},{9,... | collective-permute-start | bytes 393224 | tf_op jit(solution)/shard_map/ppermute | solution.py:41
  281.9 11.4 %collective-permute-start.46 = (bf16[32,2048]{1,0:T(8,128)(2,1)S(1)}, bf16[32,2048]{1,0:T(8,128)(2,1)S(1)}, u32[]{:S(2)}, u32[]{:S(2)}) collective-permute-start(bf16[32,2048]{1,0:T(8,128)(2,1)S(1)} %slice.343.refs_3_), channel_id=1, source_target_pairs={{0,18},{1,19},{2,16},{3,17},{4,22},{5,23},{6,20},{7,21},{8,26},{9,... | collective-permute-start | bytes 393224 | tf_op jit(solution)/shard_map/ppermute | solution.py:41
  299.7 14.1 %all-to-all-start.3 = ((bf16[4,256,128]{2,1,0:T(8,128)(2,1)}), bf16[4,256,128]{2,1,0:T(8,128)(2,1)S(1)}, u32[]{:S(2)}, u32[]{:S(2)}) async-start(bf16[4,256,128]{2,1,0:T(8,128)(2,1)} %outward.1), calls=%async_computation.3 | async-start | bytes 524288 | tf_op jit(solution)/shard_map/all_to_all | solution.py:840
  334.4 16.3 %collective-permute-start.52 = (bf16[256,2048]{1,0:T(8,128)(2,1)S(1)}, bf16[256,2048]{1,0:T(8,128)(2,1)}, u32[]{:S(2)}, u32[]{:S(2)}) collective-permute-start(bf16[256,2048]{1,0:T(8,128)(2,1)S(1)} %broadcast_add_fusion), channel_id=1, source_target_pairs={{0,1},{1,0},{2,3},{3,2},{4,5},{5,4},{6,7},{7,6},{8,9},{9,8},{10,11... | collective-permute-start | bytes 3145736 | tf_op jit(solution)/shard_map/ppermute | solution.py:41
  334.5 12.7 %collective-permute-start.63 = (bf16[2,2,256,128]{3,2,1,0:T(8,128)(2,1)}, bf16[2,2,256,128]{3,2,1,0:T(8,128)(2,1)S(1)}, u32[]{:S(2)}, u32[]{:S(2)}) collective-permute-start(bf16[2,2,256,128]{3,2,1,0:T(8,128)(2,1)} %get-tuple-element.75), channel_id=1, source_target_pairs={{0,96},{4,100},{8,104},{12,108},{16,112},{20,116},{24,120},{28,124... | collective-permute-start | bytes 786440 | tf_op jit(solution)/shard_map/ppermute | solution.py:51
  339.0 39.2 %all-to-all-start.5 = ((bf16[16,2,128,128]{3,2,1,0:T(8,128)(2,1)}), bf16[16,2,128,128]{3,2,1,0:T(8,128)(2,1)}, u32[]{:S(2)}, u32[]{:S(2)}) async-start(bf16[16,2,128,128]{3,2,1,0:T(8,128)(2,1)} %grad_output.1), calls=%async_computation.5 | async-start | bytes 2097152 | tf_op jit(solution)/shard_map/all_to_all | solution.py:898
  343.4 27.4 %collective-permute-start.59 = (bf16[2,2,256,128]{3,2,1,0:T(8,128)(2,1)}, bf16[2,2,256,128]{3,2,1,0:T(8,128)(2,1)S(1)}, u32[]{:S(2)}, u32[]{:S(2)}) collective-permute-start(bf16[2,2,256,128]{3,2,1,0:T(8,128)(2,1)} %get-tuple-element.71), channel_id=1, source_target_pairs={{0,32},{4,36},{8,40},{12,44},{16,48},{20,52},{24,56},{28,60},{32,6... | collective-permute-start | bytes 786440 | tf_op jit(solution)/shard_map/ppermute | solution.py:51
  345.2 37.5 %collective-permute-start.61 = (bf16[2,2,256,128]{3,2,1,0:T(8,128)(2,1)}, bf16[2,2,256,128]{3,2,1,0:T(8,128)(2,1)}, u32[]{:S(2)}, u32[]{:S(2)}) collective-permute-start(bf16[2,2,256,128]{3,2,1,0:T(8,128)(2,1)} %get-tuple-element.72), channel_id=1, source_target_pairs={{0,96},{4,100},{8,104},{12,108},{16,112},{20,116},{24,120},{28,124... | collective-permute-start | bytes 786440 | tf_op jit(solution)/shard_map/ppermute | solution.py:51
  346.7 37.9 %collective-permute-start.62 = (bf16[2,2,256,128]{3,2,1,0:T(8,128)(2,1)}, bf16[2,2,256,128]{3,2,1,0:T(8,128)(2,1)}, u32[]{:S(2)}, u32[]{:S(2)}) collective-permute-start(bf16[2,2,256,128]{3,2,1,0:T(8,128)(2,1)} %get-tuple-element.73), channel_id=1, source_target_pairs={{0,32},{4,36},{8,40},{12,44},{16,48},{20,52},{24,56},{28,60},{32,6... | collective-permute-start | bytes 786440 | tf_op jit(solution)/shard_map/ppermute | solution.py:51
  348.0 36.6 %collective-permute-start.64 = (bf16[2,2,256,128]{3,2,1,0:T(8,128)(2,1)}, bf16[2,2,256,128]{3,2,1,0:T(8,128)(2,1)}, u32[]{:S(2)}, u32[]{:S(2)}) collective-permute-start(bf16[2,2,256,128]{3,2,1,0:T(8,128)(2,1)} %add_convert_fusion.1), channel_id=1, source_target_pairs={{0,96},{4,100},{8,104},{12,108},{16,112},{20,116},{24,120},{28,124... | collective-permute-start | bytes 786440 | tf_op jit(solution)/shard_map/ppermute | solution.py:51
  352.8 19.6 %collective-permute-start.53 = (bf16[32,2048]{1,0:T(8,128)(2,1)S(1)}, bf16[32,2048]{1,0:T(8,128)(2,1)S(1)}, u32[]{:S(2)}, u32[]{:S(2)}) collective-permute-start(bf16[32,2048]{1,0:T(8,128)(2,1)S(1)} %get-tuple-element.127), channel_id=1, source_target_pairs={{0,18},{1,19},{2,16},{3,17},{4,22},{5,23},{6,20},{7,21},{8,26},{9,... | collective-permute-start | bytes 393224 | tf_op jit(solution)/shard_map/ppermute | solution.py:41
  372.3 15.8 %collective-permute-start.60 = (bf16[2,2,256,128]{3,2,1,0:T(8,128)(2,1)}, bf16[2,2,256,128]{3,2,1,0:T(8,128)(2,1)}, u32[]{:S(2)}, u32[]{:S(2)}) collective-permute-start(bf16[2,2,256,128]{3,2,1,0:T(8,128)(2,1)} %add_convert_fusion.3), channel_id=1, source_target_pairs={{0,32},{4,36},{8,40},{12,44},{16,48},{20,52},{24,56},{28,60},{32,6... | collective-permute-start | bytes 786440 | tf_op jit(solution)/shard_map/ppermute | solution.py:51
  377.0 19.7 %collective-permute-start.54 = (bf16[64,2048]{1,0:T(8,128)(2,1)}, bf16[64,2048]{1,0:T(8,128)(2,1)}, u32[]{:S(2)}, u32[]{:S(2)}) collective-permute-start(bf16[64,2048]{1,0:T(8,128)(2,1)} %pad_maximum_fusion.13), channel_id=1, source_target_pairs={{0,16},{1,17},{2,18},{3,19},{4,20},{5,21},{6,22},{7,23},{8,24},{9,... | collective-permute-start | bytes 786440 | tf_op jit(solution)/shard_map/ppermute | solution.py:41
  378.3 14.1 %all-to-all-start.4 = ((bf16[4,256,128]{2,1,0:T(8,128)(2,1)}), bf16[4,256,128]{2,1,0:T(8,128)(2,1)S(1)}, u32[]{:S(2)}, u32[]{:S(2)}) async-start(bf16[4,256,128]{2,1,0:T(8,128)(2,1)} %bitcast.46), calls=%async_computation.4 | async-start | bytes 524288 | tf_op jit(solution)/shard_map/all_to_all | solution.py:840
  382.6 14.0 %collective-permute-start.56 = (bf16[64,2048]{1,0:T(8,128)(2,1)}, bf16[64,2048]{1,0:T(8,128)(2,1)}, u32[]{:S(2)}, u32[]{:S(2)}) collective-permute-start(bf16[64,2048]{1,0:T(8,128)(2,1)} %pad_maximum_fusion.14), channel_id=1, source_target_pairs={{0,18},{1,19},{2,16},{3,17},{4,22},{5,23},{6,20},{7,21},{8,26},{9,... | collective-permute-start | bytes 786440 | tf_op jit(solution)/shard_map/ppermute | solution.py:41
  392.4 13.9 %all-to-all-start.6 = ((bf16[4,2,256,128]{3,2,1,0:T(8,128)(2,1)}), bf16[4,2,256,128]{3,2,1,0:T(8,128)(2,1)}, u32[]{:S(2)}, u32[]{:S(2)}) async-start(bf16[4,2,256,128]{3,2,1,0:T(8,128)(2,1)} %maximum_add_fusion), calls=%async_computation.6 | async-start | bytes 1048576 | tf_op jit(solution)/shard_map/all_to_all | solution.py:840
  418.6 11.6 %collective-permute-start.66 = (bf16[32,2048]{1,0:T(8,128)(2,1)}, bf16[32,2048]{1,0:T(8,128)(2,1)}, u32[]{:S(2)}, u32[]{:S(2)}) collective-permute-start(bf16[32,2048]{1,0:T(8,128)(2,1)} %get-tuple-element.123), channel_id=1, source_target_pairs={{0,18},{1,19},{2,16},{3,17},{4,22},{5,23},{6,20},{7,21},{8,26},{9,... | collective-permute-start | bytes 393224 | tf_op jit(solution)/shard_map/ppermute | solution.py:41
  420.0 10.2 %collective-permute-start.68 = (bf16[32,2048]{1,0:T(8,128)(2,1)}, bf16[32,2048]{1,0:T(8,128)(2,1)}, u32[]{:S(2)}, u32[]{:S(2)}) collective-permute-start(bf16[32,2048]{1,0:T(8,128)(2,1)} %get-tuple-element.122), channel_id=1, source_target_pairs={{0,16},{1,17},{2,18},{3,19},{4,20},{5,21},{6,22},{7,23},{8,24},{9,... | collective-permute-start | bytes 393224 | tf_op jit(solution)/shard_map/ppermute | solution.py:41
  426.4 51.2 %all-to-all-start.7 = ((bf16[16,6,128,128]{3,2,1,0:T(8,128)(2,1)}), bf16[16,6,128,128]{3,2,1,0:T(8,128)(2,1)S(1)}, u32[]{:S(2)}, u32[]{:S(2)}) async-start(bf16[16,6,128,128]{3,2,1,0:T(8,128)(2,1)} %grad_qkv.1), calls=%async_computation.7 | async-start | bytes 6291456 | tf_op jit(solution)/shard_map/all_to_all | solution.py:914
  432.4 9.3 %collective-permute-start.67 = (bf16[64,2048]{1,0:T(8,128)(2,1)S(1)}, bf16[64,2048]{1,0:T(8,128)(2,1)S(1)}, u32[]{:S(2)}, u32[]{:S(2)}) collective-permute-start(bf16[64,2048]{1,0:T(8,128)(2,1)S(1)} %pad_maximum_fusion.15), channel_id=1, source_target_pairs={{0,16},{1,17},{2,18},{3,19},{4,20},{5,21},{6,22},{7,23},{8,24},{9,... | collective-permute-start | bytes 786440 | tf_op jit(solution)/shard_map/ppermute | solution.py:41
  433.7 17.2 %collective-permute-start.69 = (bf16[64,2048]{1,0:T(8,128)(2,1)S(1)}, bf16[64,2048]{1,0:T(8,128)(2,1)S(1)}, u32[]{:S(2)}, u32[]{:S(2)}) collective-permute-start(bf16[64,2048]{1,0:T(8,128)(2,1)S(1)} %pad_maximum_fusion.16), channel_id=1, source_target_pairs={{0,18},{1,19},{2,16},{3,17},{4,22},{5,23},{6,20},{7,21},{8,26},{9,... | collective-permute-start | bytes 786440 | tf_op jit(solution)/shard_map/ppermute | solution.py:41
  435.6 16.0 %collective-permute-start.57 = (bf16[64,2048]{1,0:T(8,128)(2,1)}, bf16[64,2048]{1,0:T(8,128)(2,1)S(1)}, u32[]{:S(2)}, u32[]{:S(2)}) collective-permute-start(bf16[64,2048]{1,0:T(8,128)(2,1)} %fusion.14.own_ref.refs_5_), channel_id=1, source_target_pairs={{0,2},{1,3},{2,0},{3,1},{4,6},{5,7},{6,4},{7,5},{8,10},{9,11},{10,... | collective-permute-start | bytes 786440 | tf_op jit(solution)/shard_map/ppermute | solution.py:41
  451.5 8.0 %collective-permute-start.70 = (bf16[64,2048]{1,0:T(8,128)(2,1)S(1)}, bf16[64,2048]{1,0:T(8,128)(2,1)S(1)}, u32[]{:S(2)}, u32[]{:S(2)}) collective-permute-start(bf16[64,2048]{1,0:T(8,128)(2,1)S(1)} %fusion.9.own_ref), channel_id=1, source_target_pairs={{0,2},{1,3},{2,0},{3,1},{4,6},{5,7},{6,4},{7,5},{8,10},{9,11},{10,... | collective-permute-start | bytes 786440 | tf_op jit(solution)/shard_map/ppermute | solution.py:41
  452.5 10.0 %collective-permute-start.58 = (bf16[128,2048]{1,0:T(8,128)(2,1)}, bf16[128,2048]{1,0:T(8,128)(2,1)}, u32[]{:S(2)}, u32[]{:S(2)}) collective-permute-start(bf16[128,2048]{1,0:T(8,128)(2,1)} %pad_maximum_fusion.3), channel_id=1, source_target_pairs={{0,1},{1,0},{2,3},{3,2},{4,5},{5,4},{6,7},{7,6},{8,9},{9,8},{10,11... | collective-permute-start | bytes 1572872 | tf_op jit(solution)/shard_map/ppermute | solution.py:41
  462.5 11.7 %collective-permute-start.72 = (bf16[24,64,128]{2,1,0:T(8,128)(2,1)}, bf16[24,64,128]{2,1,0:T(8,128)(2,1)S(1)}, u32[]{:S(2)}, u32[]{:S(2)}) collective-permute-start(bf16[24,64,128]{2,1,0:T(8,128)(2,1)} %get-tuple-element.80), channel_id=1, source_target_pairs={{0,16},{1,17},{2,18},{3,19},{4,20},{5,21},{6,22},{7,23},{8,24},{9,... | collective-permute-start | bytes 1179656 | tf_op jit(solution)/shard_map/ppermute | solution.py:41
  482.3 9.4 %collective-permute-start.73 = (bf16[6,64,128]{2,1,0:T(8,128)(2,1)}, bf16[6,64,128]{2,1,0:T(8,128)(2,1)S(1)}, u32[]{:S(2)}, u32[]{:S(2)}) collective-permute-start(bf16[6,64,128]{2,1,0:T(8,128)(2,1)} %get-tuple-element.83), channel_id=1, source_target_pairs={{0,16},{1,17},{2,18},{3,19},{4,20},{5,21},{6,22},{7,23},{8,24},{9,... | collective-permute-start | bytes 294920 | tf_op jit(solution)/shard_map/ppermute | solution.py:41
  (88 other events, 641.7 us)
Sparse Core Ops, SparseCore 0:
  104.7 99.7 all-gather.1
  272.4 113.3 reduce-scatter.3
